TPU v7x, 256 devices: a whole 4x4x8 slice. The times are simulated.
256 devices in a mesh: dp: 16 (over z_lo, y), tensor: 16 (over z_hi, x, core).
Axes of the slice: x: 4, y: 4, z: 8 (z_hi: 2, z_lo: 4; z = z_hi * 4 + z_lo), core: 2. Of those that a mesh axis runs over, the one named last changes fastest.
Arguments:
- d_out: bfloat16 [2048, 8192], P('dp'), may hold values from -6 to 6
- gate_pre: bfloat16 [2048, 28672], P('dp', 'tensor'), may hold values from -6 to 6
- up_pre: bfloat16 [2048, 28672], P('dp', 'tensor'), may hold values from -6 to 6
- down_weight: bfloat16 [28672, 8192], P('tensor', 'dp'), may hold values from -0.03125 to 0.03125
- step_size: float32 [112, 8192], P('tensor', 'dp'), may hold values from 0.001 to 0.004
Outputs:
- d_gate: bfloat16 [2048, 28672], P('dp', 'tensor')
- d_up: bfloat16 [2048, 28672], P('dp', 'tensor')
- weight_grad: float32 [28672, 8192], P('tensor', 'dp')
- step_grad: float32 [112, 8192], P('tensor', 'dp')
All inputs are finite; a program needn't handle non-finite values.
Results may differ from a plain program's by a relative error of at most 0.025.
Values may be sent and summed in bfloat16 or wider, within the bound.
A program may use at most 128 MiB of HBM per device.

v0:
```python
import math

import jax
import jax.numpy as jnp
import numpy as np
from jax import lax
from jax.sharding import PartitionSpec as P

FF = 28672


def paley_matrix():
    digits_of = [(number % 3, number // 3 % 3, number // 9) for number in range(27)]
    lookup = {digits: number for number, digits in enumerate(digits_of)}

    def field_product(left_poly, right_poly):
        coeffs = [0, 0, 0, 0, 0]
        for left_pos in range(3):
            for right_pos in range(3):
                coeffs[left_pos + right_pos] += left_poly[left_pos] * right_poly[right_pos]
        for degree in (4, 3):
            excess = coeffs[degree]
            coeffs[degree] = 0
            coeffs[degree - 2] += excess
            coeffs[degree - 3] += 2 * excess
        return tuple((coefficient % 3 for coefficient in coeffs[:3]))

    squares_set = set((lookup[field_product(digits, digits)] for digits in digits_of[1:]))
    matrix_out = np.eye(28, dtype=np.float32)
    matrix_out[0, 1:] += 1.0
    matrix_out[1:, 0] -= 1.0
    for row_num in range(27):
        for col_num in range(27):
            if row_num != col_num:
                diff_poly = tuple(
                    (
                        (digits_of[row_num][position] - digits_of[col_num][position]) % 3
                        for position in range(3)
                    )
                )
                matrix_out[row_num + 1, col_num + 1] += (
                    1.0 if lookup[diff_poly] in squares_set else -1.0
                )
    return matrix_out


def sylvester(order_size):
    indices = np.arange(order_size)
    anded = indices[:, None] & indices[None, :]
    parity = np.zeros((order_size, order_size), np.int64)
    for bit_num in range(int(order_size).bit_length()):
        parity = parity + (anded >> bit_num & 1)
    return (1 - 2 * (parity % 2)).astype(np.float32)


def rotate_rows(tok_block, paley_table, sylvester_table, backward):
    count_rows = tok_block.shape[0]
    block_width = sylvester_table.shape[0]
    mixed_rows = jnp.dot(
        tok_block.reshape(count_rows * 28, block_width),
        jnp.asarray(sylvester_table, jnp.bfloat16),
        preferred_element_type=jnp.float32,
    )
    coupling = paley_table.T if backward else paley_table
    mixed_rows = jnp.einsum(
        "tab,ac->tcb",
        mixed_rows.reshape(count_rows, 28, block_width),
        jnp.asarray(coupling, jnp.float32),
        precision=lax.Precision.HIGHEST,
    )
    return (
        mixed_rows.reshape(count_rows, 28 * block_width) * (1.0 / math.sqrt(28 * block_width))
    ).astype(jnp.bfloat16)


def fake_quantize(weights_block, step_block):
    group_count = step_block.shape[0]
    shaped = weights_block.astype(jnp.float32).reshape(
        group_count, weights_block.shape[0] // group_count, weights_block.shape[1]
    )
    ratios = shaped / step_block[:, None, :]
    clipped = jnp.clip(ratios, -8.0, 7.0)
    turned = 2.0 * math.pi * clipped
    levels = clipped - jnp.sin(turned) / (2.0 * math.pi)
    slopes = 1.0 - jnp.cos(turned)
    quantized = (step_block[:, None, :] * levels).reshape(weights_block.shape).astype(jnp.bfloat16)
    return (quantized, ratios, levels, slopes)


def gradients_from(d_quant, ratios, levels, slopes):
    shaped = d_quant.reshape(ratios.shape)
    weight_grad = (shaped * slopes).reshape(d_quant.shape)
    step_grad = jnp.sum(shaped * (levels - ratios * slopes), axis=1) * (
        1.0 / math.sqrt(7.0 * ratios.shape[1])
    )
    return (weight_grad, step_grad)


def shards(d_out, gate_pre, up_pre, down_weight, step_size):
    gate_wide = gate_pre.astype(jnp.float32)
    up_wide = up_pre.astype(jnp.float32)
    sig = jax.nn.sigmoid(gate_wide)
    hidden = (gate_wide * sig * up_wide).astype(jnp.bfloat16)
    paley_table = paley_matrix()
    sylvester_table = sylvester(FF // 28)
    quantized, ratios, levels, slopes = fake_quantize(down_weight, step_size)
    dy_columns = lax.all_to_all(d_out, "dp", split_axis=1, concat_axis=0, tiled=True)
    spread_hidden = lax.all_to_all(hidden, "tensor", split_axis=0, concat_axis=1, tiled=True)
    turned_hidden = rotate_rows(spread_hidden, paley_table, sylvester_table, False)
    h_rot = lax.all_to_all(turned_hidden, "tensor", split_axis=1, concat_axis=0, tiled=True)
    columns = dy_columns
    d_quant = lax.dot_general(
        lax.all_gather(h_rot, "dp", axis=0, tiled=True),
        columns,
        (((0,), (0,)), ((), ())),
        preferred_element_type=jnp.float32,
    )
    columns = dy_columns
    summed = lax.psum_scatter(
        lax.dot_general(
            columns, quantized, (((1,), (1,)), ((), ())), preferred_element_type=jnp.float32
        ).astype(jnp.bfloat16),
        "dp",
        scatter_dimension=0,
        tiled=True,
    )
    spread_grad = lax.all_to_all(summed, "tensor", split_axis=0, concat_axis=1, tiled=True)
    turned_grad = rotate_rows(spread_grad, paley_table, sylvester_table, True)
    grad_hidden = lax.all_to_all(turned_grad, "tensor", split_axis=1, concat_axis=0, tiled=True)
    weight_grad, step_grad = gradients_from(d_quant, ratios, levels, slopes)
    grad_wide = grad_hidden.astype(jnp.float32)
    d_up = (grad_wide * gate_wide * sig).astype(jnp.bfloat16)
    d_gate = (grad_wide * up_wide * sig * (1.0 + gate_wide * (1.0 - sig))).astype(jnp.bfloat16)
    return (d_gate, d_up, weight_grad, step_grad)


def solution(mesh):
    return jax.shard_map(
        shards,
        mesh=mesh,
        in_specs=(
            P("dp", None),
            P("dp", "tensor"),
            P("dp", "tensor"),
            P("tensor", "dp"),
            P("tensor", "dp"),
        ),
        out_specs=(P("dp", "tensor"), P("dp", "tensor"), P("tensor", "dp"), P("tensor", "dp")),
        check_vma=False,
    )
```

profile of v0, /device:TPU:32, one launch (start us, length us, event | category | flops | bytes accessed | tf_op | source)
XLA Modules:
  0.0 414.4 jit_solution(3600354899145814468)
XLA Ops:
  7.2 0.0 copy-start.4
  7.2 3.1 copy.39
  10.3 8.7 %all-to-all-start = ((bf16[128,16,512]{2,0,1:T(8,128)(2,1)}), bf16[128,16,512]{2,0,1:T(8,128)(2,1)S(1)}, u32[]{:S(2)}, u32[]{:S(2)}) async-start(bf16[128,16,512]{2,0,1:T(8,128)(2,1)} %bitcast.57), calls=%async_computation | async-start | bytes 4194304 | tf_op jit(solution)/shard_map/all_to_all | solution.py:107
  19.0 0.0 reduce-scatter.4.cloned.1.call-start
  19.0 0.0 copy-done.4
  19.0 14.6 %fusion.2 = bf16[1792,512]{1,0:T(8,128)(2,1)} fusion(f32[7,512]{1,0:T(8,128)S(1)} %copy-done.4, bf16[1792,512]{1,0:T(8,128)(2,1)} %param.12), kind=kLoop, calls=%fused_computation.5 | loop fusion | flops 7340032 | bytes 3684352 | tf_op jit(solution)/shard_map/convert_element_type | solution.py:86
  33.6 32.6 %all-to-all-done = bf16[128,16,512]{2,0,1:T(8,128)(2,1)S(1)} async-done(((bf16[128,16,512]{2,0,1:T(8,128)(2,1)}), bf16[128,16,512]{2,0,1:T(8,128)(2,1)S(1)}, u32[]{:S(2)}, u32[]{:S(2)}) %all-to-all-start) | async-done | bytes 2097184 | tf_op jit(solution)/shard_map/all_to_all | solution.py:107
  66.2 0.0 copy-start.1
  66.2 8.3 %fusion = bf16[2048,1792]{0,1:T(8,128)(2,1)} fusion(bf16[1792,512]{1,0:T(8,128)(2,1)} %fusion.2, bf16[2048,512]{1,0:T(8,128)(2,1)S(1)} %bitcast.62), kind=kOutput, calls=%fused_computation.1 | convolution fusion | flops 3761766400 | bytes 11272192 | tf_op jit(solution)/shard_map/dot_general | solution.py:120
  74.6 0.0 copy-done.1
  74.6 10.1 %copy.35 = bf16[2048,1792]{1,0:T(8,128)(2,1)} copy(bf16[2048,1792]{0,1:T(8,128)(2,1)} %fusion) | data formatting | bytes 14680064
  84.6 0.0 copy-start
  84.6 0.0 reduce-scatter.4.cloned.1.call-update
  84.7 0.0 all-gather.2.cloned.1.call-start
  84.7 96.6 %reduce-scatter.4.cloned.1.call-done = bf16[128,1792]{1,0:T(8,128)(2,1)} async-done(((bf16[2048,1792]{1,0:T(8,128)(2,1)}), bf16[128,1792]{1,0:T(8,128)(2,1)}) %reduce-scatter.4.cloned.1.call-update) | async-done | bytes 458768 | tf_op jit(solution)/shard_map/reduce_scatter | solution.py:119
  181.3 26.0 %all_to_all.77 = bf16[16,8,1792]{2,1,0:T(8,128)(2,1)S(1)} all-to-all(bf16[16,8,1792]{2,1,0:T(8,128)(2,1)} %bitcast.68), channel_id=1, replica_groups=mesh['dp'=16,'tensor'=16] {'tensor'}, dimensions={0} | all-to-all | bytes 917504 | tf_op jit(solution)/shard_map/all_to_all | solution.py:127
  207.3 0.1 copy.30
  207.3 0.5 dot_general.27
  207.8 0.0 copy-done
  207.8 0.0 copy-start.3
  207.8 0.7 fusion.19
  208.5 1.8 fusion.7
  210.4 0.5 convert_element_type.62
  210.8 0.1 copy.31
  211.0 20.7 %all_to_all.78 = bf16[8,16,1792]{2,0,1:T(8,128)(2,1)S(1)} all-to-all(bf16[8,16,1792]{2,0,1:T(8,128)(2,1)S(1)} %copy.31), channel_id=1, replica_groups=mesh['dp'=16,'tensor'=16] {'tensor'}, dimensions={1} | all-to-all | bytes 917504 | tf_op jit(solution)/shard_map/all_to_all | solution.py:129
  231.7 0.0 copy-done.3
  231.7 2.5 fusion.18
  234.2 0.0 copy-start.5
  234.2 20.3 %all_to_all.79 = bf16[16,8,1792]{2,1,0:T(8,128)(2,1)S(1)} all-to-all(bf16[16,8,1792]{2,1,0:T(8,128)(2,1)S(1)} %get-tuple-element.6), channel_id=1, replica_groups=mesh['dp'=16,'tensor'=16] {'tensor'}, dimensions={0} | all-to-all | bytes 917504 | tf_op jit(solution)/shard_map/all_to_all | solution.py:108
  254.4 0.1 copy.32
  254.5 0.5 dot_general.30
  255.0 0.7 fusion.20
  255.7 0.0 copy-done.5
  255.7 1.1 fusion.6
  256.8 0.5 convert_element_type.73
  257.3 0.1 copy.33
  257.4 20.3 %all_to_all.80 = bf16[8,16,1792]{2,0,1:T(8,128)(2,1)} all-to-all(bf16[8,16,1792]{2,0,1:T(8,128)(2,1)S(1)} %copy.33), channel_id=1, replica_groups=mesh['dp'=16,'tensor'=16] {'tensor'}, dimensions={1} | all-to-all | bytes 917504 | tf_op jit(solution)/shard_map/all_to_all | solution.py:110
  277.7 0.0 all-gather.2.cloned.1.call-update
  277.7 86.6 %all-gather.2.cloned.1.call-done = bf16[2048,1792]{1,0:T(8,128)(2,1)} async-done(((bf16[128,1792]{1,0:T(8,128)(2,1)}), bf16[2048,1792]{1,0:T(8,128)(2,1)}) %all-gather.2.cloned.1.call-update) | async-done | bytes 7340048 | tf_op jit(solution)/shard_map/all_gather | solution.py:113
  364.3 0.0 copy-start.2
  364.3 10.4 %copy.34 = bf16[1792,2048]{1,0:T(8,128)(2,1)} copy(bf16[1792,2048]{0,1:T(8,128)(2,1)} %bitcast.58) | data formatting | bytes 14680064 | tf_op jit(solution)/shard_map/dot_general | solution.py:112
  374.7 0.0 copy-done.2
  374.7 19.1 %multiply_reduce_fusion = (f32[7,512]{1,0:T(8,128)S(1)}, f32[7,256,512]{2,1,0:T(8,128)S(1)}, f32[7,256,512]{2,1,0:T(8,128)S(1)}) fusion(f32[7,512]{1,0:T(8,128)S(1)} %copy-done.4, bf16[7,256,512]{2,1,0:T(8,128)(2,1)} %bitcast.64, bf16[7,256,2048]{2,1,0:T(8,128)(2,1)} %bitcast.59, bf16[2048,512,1]{1,0,2:T(8,128)(2,1)S(1)} %bitcast.63), kind=kOutput, calls=%fused_computation.6 | convolution fusion | flops 3768185344 | bytes 18640896 | tf_op jit(solution)/shard_map/dot_general | solution.py:112
  393.8 0.6 broadcast_multiply_fusion
  394.5 13.1 %fusion.3 = f32[7,256,512]{2,1,0:T(8,128)} fusion(f32[7,256,512]{2,1,0:T(8,128)S(1)} %get-tuple-element.9, f32[7,256,512]{2,1,0:T(8,128)S(1)} %get-tuple-element.5, f32[7,512]{1,0:T(8,128)S(1)} %copy-done.4), kind=kLoop, calls=%fused_computation.8 | loop fusion | flops 4587520 | bytes 11024384 | tf_op jit(solution)/shard_map/mul | solution.py:92
Async XLA Ops:
  7.2 11.9 %copy-start.4 = (f32[7,512]{1,0:T(8,128)S(1)}, f32[7,512]{1,0:T(8,128)}, u32[]{:S(2)}) copy-start(f32[7,512]{1,0:T(8,128)} %param.13) | copy-start | bytes 43012
  10.3 55.9 %all-to-all-start = ((bf16[128,16,512]{2,0,1:T(8,128)(2,1)}), bf16[128,16,512]{2,0,1:T(8,128)(2,1)S(1)}, u32[]{:S(2)}, u32[]{:S(2)}) async-start(bf16[128,16,512]{2,0,1:T(8,128)(2,1)} %bitcast.57), calls=%async_computation | async-start | bytes 4194304 | tf_op jit(solution)/shard_map/all_to_all | solution.py:107
  19.0 162.3 %reduce-scatter.4.cloned.1.call-start = ((), (), s32[]{:S(2)}) async-start(), calls=%async_computation.7 | async-start | bytes 7798784 | tf_op jit(solution)/shard_map/reduce_scatter | solution.py:119
  66.2 8.3 %copy-start.1 = (bf16[128,16,512]{2,0,1:T(8,128)(2,1)}, bf16[128,16,512]{2,0,1:T(8,128)(2,1)S(1)}, u32[]{:S(2)}) copy-start(bf16[128,16,512]{2,0,1:T(8,128)(2,1)S(1)} %all-to-all-done) | copy-start | bytes 6291460
  84.6 123.2 %copy-start = (bf16[1024,1024,1]{1,0,2:T(8,128)(2,1)S(1)}, bf16[1024,1024,1]{1,0,2:T(8,128)(2,1)}, u32[]{:S(2)}) copy-start(bf16[1024,1024,1]{1,0,2:T(8,128)(2,1)} %constant.27) | copy-start | bytes 6291460
  84.7 279.6 %all-gather.2.cloned.1.call-start = ((), (), s32[]{:S(2)}) async-start(), calls=%async_computation.6 | async-start | bytes 7798784 | tf_op jit(solution)/shard_map/all_gather | solution.py:113
  207.8 23.8 %copy-start.3 = (bf16[128,1792]{1,0:T(8,128)(2,1)S(1)}, bf16[128,1792]{1,0:T(8,128)(2,1)}, u32[]{:S(2)}) copy-start(bf16[128,1792]{1,0:T(8,128)(2,1)} %param.11) | copy-start | bytes 1376260
  234.2 21.5 %copy-start.5 = (f32[28,28,1]{0,1,2:T(8,128)S(1)}, f32[28,28,1]{0,1,2:T(8,128)}, u32[]{:S(2)}) copy-start(f32[28,28,1]{0,1,2:T(8,128)} %constant.29) | copy-start | bytes 9412
  364.3 10.4 %copy-start.2 = (bf16[128,16,512]{2,0,1:T(8,128)(2,1)S(1)}, bf16[128,16,512]{2,0,1:T(8,128)(2,1)}, u32[]{:S(2)}) copy-start(bf16[128,16,512]{2,0,1:T(8,128)(2,1)} %copy-done.1) | copy-start | bytes 6291460
Sparse Core Ops, SparseCore 0:
  84.8 96.4 reduce-scatter.3
  277.9 86.4 all-gather.1
where the time goes:
time: 421 us; the launch traced here: 414 us
  waiting for transfers between devices  216 us (51%)
  blocking collectives  87.2 us (21%)
  matrix products  31.7 us (8%)
  other arithmetic  30.8 us (7%)
  local copies, waits for them, and re-layouts  26 us (6%)
  between operations  14.2 us (3%)
  starting transfers between devices  8.73 us (2%)
    reduce_scatter x1, waiting for transfers between devices, shards(): lax.psum_scatter(lax.dot_general(columns, quantized, (((1,), (1,)), ((),...  96.6 us
    all_gather x1, waiting for transfers between devices, shards(): lax.all_gather(h_rot, 'dp', axis=0, tiled=True)  86.6 us
    all_to_all x1, waiting for transfers between devices, shards(): lax.all_to_all(d_out, 'dp', split_axis=1, concat_axis=0, tiled=True)  32.6 us
    all_to_all x1, blocking collectives, shards(): lax.all_to_all(summed, 'tensor', split_axis=0, concat_axis=1, tiled=True)  26 us
    all_to_all x1, blocking collectives, shards(): lax.all_to_all(turned_grad, 'tensor', split_axis=1, concat_axis=0, tiled=...  20.7 us
    all_to_all x1, blocking collectives, shards(): lax.all_to_all(turned_hidden, 'tensor', split_axis=1, concat_axis=0, tile...  20.3 us
    all_to_all x1, blocking collectives, shards(): lax.all_to_all(hidden, 'tensor', split_axis=0, concat_axis=1, tiled=True)  20.3 us
    dot_general x1, matrix products, shards(): lax.dot_general(lax.all_gather(h_rot, 'dp', axis=0, tiled=True), columns,...  19.1 us
  transfers between devices with their start and end apart: 3, of which 3 were waited for; matrix products, arithmetic and copies ran while one was open for 4% of the time, Pallas kernels for 0%

commit v1 on v0

v1 whole, which is shorter than its diff:
```python
import functools
import math

import jax
import jax.numpy as jnp
import numpy as np
from jax import lax
from jax.experimental import pallas as pl
from jax.experimental.pallas import tpu as pltpu
from jax.sharding import PartitionSpec as P

FF = 28672
F32, BF16 = jnp.float32, jnp.bfloat16
MESH = pl.DeviceIdType.MESH
SCALE = 1.0 / math.sqrt(FF)


def paley_matrix():
    digits_of = [(number % 3, number // 3 % 3, number // 9) for number in range(27)]
    lookup = {digits: number for number, digits in enumerate(digits_of)}

    def field_product(left_poly, right_poly):
        coeffs = [0, 0, 0, 0, 0]
        for left_pos in range(3):
            for right_pos in range(3):
                coeffs[left_pos + right_pos] += left_poly[left_pos] * right_poly[right_pos]
        for degree in (4, 3):
            excess = coeffs[degree]
            coeffs[degree] = 0
            coeffs[degree - 2] += excess
            coeffs[degree - 3] += 2 * excess
        return tuple((coefficient % 3 for coefficient in coeffs[:3]))

    squares_set = set((lookup[field_product(digits, digits)] for digits in digits_of[1:]))
    matrix_out = np.eye(28, dtype=np.float32)
    matrix_out[0, 1:] += 1.0
    matrix_out[1:, 0] -= 1.0
    for row_num in range(27):
        for col_num in range(27):
            if row_num != col_num:
                diff_poly = tuple(
                    (
                        (digits_of[row_num][position] - digits_of[col_num][position]) % 3
                        for position in range(3)
                    )
                )
                matrix_out[row_num + 1, col_num + 1] += (
                    1.0 if lookup[diff_poly] in squares_set else -1.0
                )
    return matrix_out


def sylvester(order_size):
    indices = np.arange(order_size)
    anded = indices[:, None] & indices[None, :]
    parity = np.zeros((order_size, order_size), np.int64)
    for bit_num in range(int(order_size).bit_length()):
        parity = parity + (anded >> bit_num & 1)
    return (1 - 2 * (parity % 2)).astype(np.float32)


def half_turn_series():
    points = 0.125 - 0.125 * np.cos((np.arange(64) + 0.5) * np.pi / 64)
    root = np.sqrt(points)
    a = np.polyfit(points, np.sin(np.pi * root) / root, 5)
    b = np.polyfit(points, np.cos(np.pi * root), 6)
    return [float(v) for v in a], [float(v) for v in b]


def horner(coefficients, u):
    total = coefficients[0] * u + coefficients[1]
    for c in coefficients[2:]:
        total = total * u + c
    return total


def dot(a, b, ca, cb):
    return lax.dot_general(a, b, (((ca,), (cb,)), ((), ())), preferred_element_type=F32)


def mix_paley(paley, src, dst, scale):
    def step(b, carry):
        for half in range(2):
            rows = slice(8 * half, 8 * half + 8)
            x = [src[b, a, rows, :] for a in range(28)]
            whole = x
            while len(whole) > 1:
                whole = [whole[i] + whole[i + 1] if i + 1 < len(whole) else whole[i] for i in range(0, len(whole), 2)]
            for c in range(28):
                negative = [x[a] for a in range(28) if paley[a, c] < 0]
                if negative:
                    less = negative[0]
                    for n in negative[1:]:
                        less = less + n
                    src[4 + b, c, rows, :] = (whole[0] - 2.0 * less) * scale
                else:
                    src[4 + b, c, rows, :] = whole[0] * scale
        for c in range(28):
            dst[c * 4 + b] = src[4 + b, c].astype(BF16)
        return carry

    lax.fori_loop(0, 4, step, 0)


def kernel(
    dy_ref, gate_ref, up_ref, dw_ref, step_ref, h256_ref,
    dgate_ref, dup_ref, wg_ref, sg_ref,
    hid, hs, h1, mixf, h2, hb, dyb, qb, slopes, extra, gsend, gx, gsum, gr, gm, fr, gh, dsend, dx,
    s_loc, s_h1s, s_h1r, s_h2s, s_h2r, s_hxs, s_hxr, s_d1s, s_d1r, s_d2s, s_d2r, s_qs, s_qr,
    s_gxs, s_gxr, s_grs, s_grr, s_fs, s_fr, s_xs, s_xr,
):
    paley = paley_matrix()
    sin_series, cos_series = half_turn_series()
    d, t = lax.axis_index("dp"), lax.axis_index("tensor")
    z, y = d // 4, d % 4
    yi = y % 2
    yo = 1 - yi
    d_t = z * 4 + y + 1 - 2 * yi
    d_c = z * 4 + 3 - y
    di = y // 2
    do = 1 - di
    tg, lh = t // 2, t % 2
    part = t % 8
    hi8 = t - part

    def remote(src, dst, ss, rs, dev_d, dev_t):
        return pltpu.make_async_remote_copy(
            src_ref=src, dst_ref=dst, send_sem=ss, recv_sem=rs, device_id=(dev_d, dev_t), device_id_type=MESH
        )

    def await_bytes(ref, sem):
        pltpu.make_async_copy(ref, ref, sem).wait()

    def rows16(i):
        return pl.ds(pl.multiple_of(i * 16, 16), 16)

    def peer64(j):
        return lax.rem(z + j % 4, 4) , lax.rem(t + j // 4, 16)

    barrier = pltpu.get_barrier_semaphore()

    def greet(j, carry):
        zz, tt = peer64(j)
        pl.semaphore_signal(barrier, inc=1, device_id=(zz * 4 + y, tt), device_id_type=MESH)
        return carry

    lax.fori_loop(1, 64, greet, 0)
    for zz in range(4):
        pl.semaphore_signal(barrier, inc=1, device_id=(zz * 4 + y + 1 - 2 * yi, t), device_id_type=MESH)
    pl.semaphore_signal(barrier, inc=1, device_id=(d_c, t), device_id_type=MESH)

    def hidden_step(i, carry):
        rows = rows16(i)
        for q in range(7):
            cols = slice(256 * q, 256 * q + 256)
            g = gate_ref[rows, cols].astype(F32)
            u = up_ref[rows, cols].astype(F32)
            hid[rows, cols] = (g * jax.nn.sigmoid(g) * u).astype(BF16)
        return carry

    lax.fori_loop(0, 8, hidden_step, 0)
    for q in range(7):
        turned = dot(hid[:, 256 * q : 256 * q + 256], h256_ref[...], 1, 0).astype(BF16)
        hs[0, q] = turned[:, :128]
        hs[1, q] = turned[:, 128:]

    pl.semaphore_wait(barrier, 68)

    def send_h1(k, carry):
        p = lax.rem(t + k, 16)
        remote(hs.at[p % 2, :, rows16(p // 2), :], h1.at[pl.ds(7 * t, 7)], s_h1s, s_h1r, d, p).start()
        return carry

    pltpu.make_async_copy(hs.at[lh, :, rows16(tg), :], h1.at[pl.ds(7 * t, 7)], s_h1r).start()
    lax.fori_loop(1, 16, send_h1, 0)

    def columns(zz, yy, c):
        low = yy - (yy // 2) * (2 * yy - 3)
        return pl.ds(pl.multiple_of(512 * (zz * 4 + low + c * (3 - 2 * low)), 512), 512)

    def send_d1(j, carry):
        zz = lax.rem(z + j // 2, 4)
        yy = y - yi + lax.rem(yi + j % 2, 2)
        for c in range(2):
            remote(
                dy_ref.at[rows16(part), columns(zz, yy, c)],
                dyb.at[yi, z, rows16(part), pl.ds(512 * c, 512)],
                s_d1s, s_d1r, zz * 4 + yy, t,
            ).start()
        return carry

    for c in range(2):
        pltpu.make_async_copy(
            dy_ref.at[rows16(part), columns(z, y, c)], dyb.at[yi, z, rows16(part), pl.ds(512 * c, 512)], s_d1r
        ).start()
    lax.fori_loop(1, 8, send_d1, 0)

    def quant_group(g, carry):
        step = step_ref[pl.ds(g, 1), :]
        inverse = 1.0 / step

        def chunk(i, inner):
            rows = rows16(g * 16 + i)
            ratios = dw_ref[rows, :].astype(F32) * inverse
            clipped = jnp.clip(ratios, -8.0, 7.0)
            r = clipped - jnp.round(clipped)
            u = r * r
            s = r * horner(sin_series, u)
            c = horner(cos_series, u)
            levels = clipped - s * c * (1.0 / math.pi)
            slope = 2.0 * s * s
            slopes[rows, :] = slope
            extra[rows, :] = levels - ratios * slope
            qb[di, g, rows16(i), :] = (step * levels).astype(BF16)
            return inner

        lax.fori_loop(0, 16, chunk, 0)
        remote(qb.at[di, g], qb.at[di, g], s_qs.at[g], s_qr.at[g], d_c, t).start()
        return carry

    lax.fori_loop(0, 7, quant_group, 0)

    await_bytes(dyb.at[0, :, 0:32, :], s_d1r)

    def send_d2(k, carry):
        p = hi8 + lax.rem(part + k, 8)
        block = dyb.at[:, :, rows16(part), :]
        remote(block, block, s_d2s, s_d2r, d, p).start()
        return carry

    lax.fori_loop(1, 8, send_d2, 0)

    await_bytes(h1, s_h1r)

    def spread_h(a, carry):
        x = [h1[a * 4 + b].astype(F32) for b in range(4)]
        p0, p1, m0, m1 = x[0] + x[1], x[2] + x[3], x[0] - x[1], x[2] - x[3]
        mixf[0, a] = p0 + p1
        mixf[1, a] = m0 + m1
        mixf[2, a] = p0 - p1
        mixf[3, a] = m0 - m1
        return carry

    lax.fori_loop(0, 28, spread_h, 0)
    mix_paley(paley, mixf, h2, SCALE)

    def h_place(zz, ti):
        return hb.at[yi, ti % 2, :, pl.ds(pl.multiple_of(zz * 128 + (ti // 2) * 16, 16), 16), :]

    def send_h2(j, carry):
        zz, tt = peer64(j)
        remote(h2.at[pl.ds(7 * tt, 7)], h_place(z, t), s_h2s, s_h2r.at[z], zz * 4 + y, tt).start()
        return carry

    pltpu.make_async_copy(h2.at[pl.ds(7 * t, 7)], h_place(z, t), s_h2r.at[z]).start()
    lax.fori_loop(1, 64, send_h2, 0)

    await_bytes(dyb.at[:, :, 0:112, :], s_d2r)

    def product_g(which, g):
        total = dot(dyb[which, :, :, :512].reshape(512, 512), qb[0, g], 1, 1)
        return total + dot(dyb[which, :, :, 512:].reshape(512, 512), qb[1, g], 1, 1)

    def grad_group(g, carry):
        remote(qb.at[di, g], qb.at[do, g], s_qs.at[g], s_qr.at[g], d_c, t).wait_recv()
        theirs = product_g(yo, g).astype(BF16)
        gsend[g, 0] = theirs[:, :128]
        gsend[g, 1] = theirs[:, 128:]
        remote(gsend.at[g], gx.at[g], s_gxs.at[g], s_gxr.at[g], d_t, t).start()
        ours = product_g(yi, g).astype(BF16)
        gsum[0, g] = ours[:, :128]
        gsum[1, g] = ours[:, 128:]
        return carry

    lax.fori_loop(0, 7, grad_group, 0)

    def add_group(g, carry):
        remote(gsend.at[g], gx.at[g], s_gxs.at[g], s_gxr.at[g], d_t, t).wait_recv()

        def chunk(i, inner):
            rows = pl.ds(pl.multiple_of(i * 64, 64), 64)
            for k in range(2):
                gsum[k, g, rows, :] = (gsum[k, g, rows, :].astype(F32) + gx[g, k, rows, :].astype(F32)).astype(BF16)
            return inner

        return lax.fori_loop(0, 8, chunk, carry)

    lax.fori_loop(0, 7, add_group, 0)

    def g_piece(zz, ti):
        return gsum.at[ti % 2, :, pl.ds(pl.multiple_of(zz * 128 + (ti // 2) * 16, 16), 16), :]

    def g_place(zz, ti):
        return gr.at[pl.ds(zz * 112 + 7 * ti, 7)]

    def send_gr(j, carry):
        zz, tt = peer64(j)
        remote(g_piece(zz, tt), g_place(z, t), s_grs, s_grr, zz * 4 + y, tt).start()
        return carry

    pltpu.make_async_copy(g_piece(z, t), g_place(z, t), s_grr).start()
    lax.fori_loop(1, 64, send_gr, 0)

    def h_block(which, zz):
        return hb.at[which, :, :, pl.ds(pl.multiple_of(zz * 128, 128), 128), :]

    def forward_h(k, carry):
        zz = lax.rem(z + k, 4)
        await_bytes(h_block(yi, zz), s_h2r.at[zz])
        remote(h_block(yi, zz), h_block(yi, zz), s_hxs.at[k], s_hxr.at[k], d_t, t).start()
        return carry

    lax.fori_loop(0, 4, forward_h, 0)

    def receive_h(k, carry):
        zz = lax.rem(z + k, 4)
        remote(h_block(yi, zz), h_block(yo, zz), s_hxs.at[k], s_hxr.at[k], d_t, t).wait_recv()
        return carry

    lax.fori_loop(0, 4, receive_h, 0)

    def product_d(q, half, c):
        cols = pl.ds(pl.multiple_of(c * 512, 512), 512)
        total = dot(hb[0, half, q], dyb[0, :, :, cols].reshape(512, 512), 0, 0)
        return total + dot(hb[1, half, q], dyb[1, :, :, cols].reshape(512, 512), 0, 0)

    def weight_group(q, carry):
        for half in range(2):
            dsend[q, 128 * half : 128 * half + 128, :] = product_d(q, half, do).astype(BF16)
        remote(dsend.at[q], dx.at[q], s_xs.at[q], s_xr.at[q], d_c, t).start()
        for half in range(2):
            wg_ref[pl.ds(pl.multiple_of(q * 256 + 128 * half, 128), 128), :] = product_d(q, half, di)
        return carry

    lax.fori_loop(0, 7, weight_group, 0)

    await_bytes(gr, s_grr)

    def spread_g(a, carry):
        x = []
        for b in range(4):
            total = gr[a * 4 + b].astype(F32)
            for zz in range(1, 4):
                total = total + gr[112 * zz + a * 4 + b].astype(F32)
            x.append(total)
        p0, p1, m0, m1 = x[0] + x[1], x[2] + x[3], x[0] - x[1], x[2] - x[3]
        mixf[0, a] = p0 + p1
        mixf[1, a] = m0 + m1
        mixf[2, a] = p0 - p1
        mixf[3, a] = m0 - m1
        return carry

    lax.fori_loop(0, 28, spread_g, 0)
    mix_paley(paley.T, mixf, gm, SCALE)

    def f_place(ti):
        return fr.at[ti % 2, :, rows16(ti // 2), :]

    def send_f(k, carry):
        p = lax.rem(t + k, 16)
        remote(gm.at[pl.ds(7 * p, 7)], f_place(t), s_fs, s_fr, d, p).start()
        return carry

    pltpu.make_async_copy(gm.at[pl.ds(7 * t, 7)], f_place(t), s_fr).start()
    lax.fori_loop(1, 16, send_f, 0)
    await_bytes(fr, s_fr)

    for q in range(7):
        gh[...] = dot(fr[0, q], h256_ref[:128, :], 1, 0) + dot(fr[1, q], h256_ref[128:, :], 1, 0)
        cols = slice(256 * q, 256 * q + 256)

        def finish(i, carry, cols=cols):
            rows = rows16(i)
            g = gate_ref[rows, cols].astype(F32)
            u = up_ref[rows, cols].astype(F32)
            sig = jax.nn.sigmoid(g)
            grad = gh[rows, :] * sig
            dup_ref[rows, cols] = (grad * g).astype(BF16)
            dgate_ref[rows, cols] = (grad * u * (1.0 + g * (1.0 - sig))).astype(BF16)
            return carry

        lax.fori_loop(0, 8, finish, 0)

    def weight_finish(q, carry):
        remote(dsend.at[q], dx.at[q], s_xs.at[q], s_xr.at[q], d_c, t).wait_recv()

        def chunk(i, acc):
            rows = rows16(q * 16 + i)
            total = wg_ref[rows, :] + dx[q, rows16(i), :].astype(F32)
            wg_ref[rows, :] = total * slopes[rows, :]
            return acc + total * extra[rows, :]

        acc = lax.fori_loop(0, 16, chunk, jnp.zeros((16, 512), F32))
        sg_ref[pl.ds(q, 1), :] = jnp.sum(acc, axis=0, keepdims=True) * (1.0 / math.sqrt(1792.0))
        return carry

    lax.fori_loop(0, 7, weight_finish, 0)

    await_bytes(h1.at[0:105], s_h1s)
    await_bytes(gr.at[0:441], s_h2s)
    await_bytes(gr.at[0:441], s_grs)
    await_bytes(gm.at[0:105], s_fs)
    await_bytes(dyb.at[0, 0, 0:112, :], s_d1s)
    await_bytes(dyb.at[:, :, 0:112, :], s_d2s)

    def drain7(g, carry):
        remote(qb.at[di, g], qb.at[di, g], s_qs.at[g], s_qr.at[g], d_c, t).wait_send()
        remote(gsend.at[g], gx.at[g], s_gxs.at[g], s_gxr.at[g], d_t, t).wait_send()
        remote(dsend.at[g], dx.at[g], s_xs.at[g], s_xr.at[g], d_c, t).wait_send()
        return carry

    lax.fori_loop(0, 7, drain7, 0)

    def drain4(k, carry):
        zz = lax.rem(z + k, 4)
        remote(h_block(yi, zz), h_block(yi, zz), s_hxs.at[k], s_hxr.at[k], d_t, t).wait_send()
        return carry

    lax.fori_loop(0, 4, drain4, 0)


def shards(d_out, gate_pre, up_pre, down_weight, step_size):
    h256 = jnp.asarray(sylvester(256), BF16)
    vmem = pl.BlockSpec(memory_space=pltpu.VMEM)
    dma = pltpu.SemaphoreType.DMA
    return pl.pallas_call(
        kernel,
        out_shape=(
            jax.ShapeDtypeStruct((128, 1792), BF16),
            jax.ShapeDtypeStruct((128, 1792), BF16),
            jax.ShapeDtypeStruct((1792, 512), F32),
            jax.ShapeDtypeStruct((7, 512), F32),
        ),
        in_specs=[pl.BlockSpec(memory_space=pl.ANY)] + [vmem] * 5,
        out_specs=(vmem,) * 4,
        scratch_shapes=[
            pltpu.VMEM((128, 1792), BF16),
            pltpu.VMEM((2, 7, 128, 128), BF16),
            pltpu.VMEM((112, 16, 128), BF16),
            pltpu.VMEM((8, 28, 16, 128), F32),
            pltpu.VMEM((112, 16, 128), BF16),
            pltpu.VMEM((2, 2, 7, 512, 128), BF16),
            pltpu.VMEM((2, 4, 128, 1024), BF16),
            pltpu.VMEM((2, 7, 256, 512), BF16),
            pltpu.VMEM((1792, 512), F32),
            pltpu.VMEM((1792, 512), F32),
            pltpu.VMEM((7, 2, 512, 128), BF16),
            pltpu.VMEM((7, 2, 512, 128), BF16),
            pltpu.VMEM((2, 7, 512, 128), BF16),
            pltpu.VMEM((448, 16, 128), BF16),
            pltpu.VMEM((112, 16, 128), BF16),
            pltpu.VMEM((2, 7, 128, 128), BF16),
            pltpu.VMEM((128, 256), F32),
            pltpu.VMEM((7, 256, 512), BF16),
            pltpu.VMEM((7, 256, 512), BF16),
            dma,
            dma, dma,
            dma, dma((4,)),
            dma((4,)), dma((4,)),
            dma, dma,
            dma, dma,
            dma((7,)), dma((7,)),
            dma((7,)), dma((7,)),
            dma, dma,
            dma, dma,
            dma((7,)), dma((7,)),
        ],
        compiler_params=pltpu.CompilerParams(
            collective_id=0, has_side_effects=True, vmem_limit_bytes=58 * 1024 * 1024
        ),
        cost_estimate=pl.CostEstimate(flops=8_000_000_000, bytes_accessed=12_000_000, transcendentals=1_000_000),
    )(d_out, gate_pre, up_pre, down_weight, step_size, h256)


def solution(mesh):
    return jax.shard_map(
        shards,
        mesh=mesh,
        in_specs=(
            P("dp", None),
            P("dp", "tensor"),
            P("dp", "tensor"),
            P("tensor", "dp"),
            P("tensor", "dp"),
        ),
        out_specs=(P("dp", "tensor"), P("dp", "tensor"), P("tensor", "dp"), P("tensor", "dp")),
        check_vma=False,
    )
```

time: 421 us -> 200 us (0.48)
  the two profiles are of different devices: /device:TPU:32 before, /device:TPU:69 now
where the time goes in v1:
time: 200 us; the launch traced here: 199 us
  Pallas kernels  190 us (95%)
  local copies, waits for them, and re-layouts  8.5 us (4%)
    pallas_call x1, Pallas kernels, shards(): pl.pallas_call(kernel, out_shape=(jax.ShapeDtypeStruct((128, 1792), BF16)...  190 us
    unnamed x6, local copies, waits for them, and re-layouts  8.5 us

profile of v1, /device:TPU:69, one launch (start us, length us, event | category | flops | bytes accessed | tf_op | source)
XLA Modules:
  0.0 199.3 jit_solution(5493233030853969579)
XLA Ops:
  0.6 190.2 %shard_map.93 = (bf16[128,1792]{1,0:T(8,128)(2,1)}, bf16[128,1792]{1,0:T(8,128)(2,1)}, f32[1792,512]{1,0:T(8,128)}, f32[7,512]{1,0:T(8,128)}) custom-call(bf16[128,8192]{1,0:T(8,128)(2,1)} %dy_ref.1, bf16[128,1792]{1,0:T(8,128)(2,1)} %gate_ref.1, bf16[128,1792]{1,0:T(8,128)(2,1)} %up_ref.1, bf16[1792,512]{1,0:T(8,128)(2,1)} %dw_ref.1, f32[7,512]{1,0:T(8,128)} %step_ref.1, ...), custom_call_target="tpu_custom_call" | custom-call | flops 8000000000 | bytes 12000000 | tf_op jit(solution)/shard_map/pallas_call | solution.py:426
  190.8 1.8 copy.14
  192.6 1.8 copy.15
  194.4 0.0 copy-start
  194.4 4.3 %copy.16 = f32[1792,512]{1,0:T(8,128)} copy(f32[1792,512]{1,0:T(8,128)} %get-tuple-element.10) | data formatting | bytes 7340032
  198.7 0.0 copy-done
  198.7 0.6 copy.17
Async XLA Ops:
  194.4 4.3 %copy-start = (f32[7,512]{1,0:T(8,128)S(1)}, f32[7,512]{1,0:T(8,128)}, u32[]{:S(2)}) copy-start(f32[7,512]{1,0:T(8,128)} %get-tuple-element.11) | copy-start | bytes 43012

commit v2 on v1

--- a/solution.py
+++ b/solution.py
@@ -1,4 +1,3 @@
-import functools
 import math
 
 import jax
@@ -13,6 +12,7 @@
 F32, BF16 = jnp.float32, jnp.bfloat16
 MESH = pl.DeviceIdType.MESH
 SCALE = 1.0 / math.sqrt(FF)
+CHUNKS = ((0, 4), (4, 3))
 
 
 def paley_matrix():
@@ -104,9 +104,9 @@
 
 def kernel(
     dy_ref, gate_ref, up_ref, dw_ref, step_ref, h256_ref,
-    dgate_ref, dup_ref, wg_ref, sg_ref,
-    hid, hs, h1, mixf, h2, hb, dyb, qb, slopes, extra, gsend, gx, gsum, gr, gm, fr, gh, dsend, dx,
-    s_loc, s_h1s, s_h1r, s_h2s, s_h2r, s_hxs, s_hxr, s_d1s, s_d1r, s_d2s, s_d2r, s_qs, s_qr,
+    fr, wg_ref, sg_ref,
+    hid, hs, h1, mixf, h2, hb, dyb, qb, slopes, extra, gsend, gx, gsum, gr, gm, dsend, dx,
+    s_h1s, s_h1r, s_h2s, s_h2r, s_hxs, s_hxr, s_d1s, s_d1r, s_d2s, s_d2r, s_d3s, s_d3r, s_qs, s_qr,
     s_gxs, s_gxr, s_grs, s_grr, s_fs, s_fr, s_xs, s_xr,
 ):
     paley = paley_matrix()
@@ -166,14 +166,6 @@
 
     pl.semaphore_wait(barrier, 68)
 
-    def send_h1(k, carry):
-        p = lax.rem(t + k, 16)
-        remote(hs.at[p % 2, :, rows16(p // 2), :], h1.at[pl.ds(7 * t, 7)], s_h1s, s_h1r, d, p).start()
-        return carry
-
-    pltpu.make_async_copy(hs.at[lh, :, rows16(tg), :], h1.at[pl.ds(7 * t, 7)], s_h1r).start()
-    lax.fori_loop(1, 16, send_h1, 0)
-
     def columns(zz, yy, c):
         low = yy - (yy // 2) * (2 * yy - 3)
         return pl.ds(pl.multiple_of(512 * (zz * 4 + low + c * (3 - 2 * low)), 512), 512)
@@ -194,6 +186,14 @@
             dy_ref.at[rows16(part), columns(z, y, c)], dyb.at[yi, z, rows16(part), pl.ds(512 * c, 512)], s_d1r
         ).start()
     lax.fori_loop(1, 8, send_d1, 0)
+
+    def send_h1(k, carry):
+        p = lax.rem(t + k, 16)
+        remote(hs.at[p % 2, :, rows16(p // 2), :], h1.at[pl.ds(7 * t, 7)], s_h1s, s_h1r, d, p).start()
+        return carry
+
+    pltpu.make_async_copy(hs.at[lh, :, rows16(tg), :], h1.at[pl.ds(7 * t, 7)], s_h1r).start()
+    lax.fori_loop(1, 16, send_h1, 0)
 
     def quant_group(g, carry):
         step = step_ref[pl.ds(g, 1), :]
@@ -222,13 +222,18 @@
 
     await_bytes(dyb.at[0, :, 0:32, :], s_d1r)
 
+    sibling = t + 1 - 2 * lh
+
+    def d2_block(k):
+        return dyb.at[:, :, rows16(lax.rem(part + 2 * k, 8)), :]
+
     def send_d2(k, carry):
-        p = hi8 + lax.rem(part + k, 8)
-        block = dyb.at[:, :, rows16(part), :]
-        remote(block, block, s_d2s, s_d2r, d, p).start()
-        return carry
-
-    lax.fori_loop(1, 8, send_d2, 0)
+        p = hi8 + lax.rem(part + 2 * k, 8)
+        remote(d2_block(0), d2_block(0), s_d2s, s_d2r.at[k], d, p).start()
+        return carry
+
+    lax.fori_loop(1, 4, send_d2, 0)
+    remote(d2_block(0), d2_block(0), s_d3s, s_d3r, d, sibling).start()
 
     await_bytes(h1, s_h1r)
 
@@ -244,18 +249,35 @@
     lax.fori_loop(0, 28, spread_h, 0)
     mix_paley(paley, mixf, h2, SCALE)
 
-    def h_place(zz, ti):
-        return hb.at[yi, ti % 2, :, pl.ds(pl.multiple_of(zz * 128 + (ti // 2) * 16, 16), 16), :]
-
-    def send_h2(j, carry):
-        zz, tt = peer64(j)
-        remote(h2.at[pl.ds(7 * tt, 7)], h_place(z, t), s_h2s, s_h2r.at[z], zz * 4 + y, tt).start()
-        return carry
-
-    pltpu.make_async_copy(h2.at[pl.ds(7 * t, 7)], h_place(z, t), s_h2r.at[z]).start()
-    lax.fori_loop(1, 64, send_h2, 0)
-
-    await_bytes(dyb.at[:, :, 0:112, :], s_d2r)
+    def h_place(zz, ti, chunk):
+        q0, n = CHUNKS[chunk]
+        return hb.at[yi, ti % 2, q0 : q0 + n, pl.ds(pl.multiple_of(zz * 128 + (ti // 2) * 16, 16), 16), :]
+
+    def push_h(chunk):
+        q0, n = CHUNKS[chunk]
+
+        def send_h2(j, carry):
+            zz, tt = peer64(j)
+            remote(
+                h2.at[pl.ds(7 * tt + q0, n)], h_place(z, t, chunk), s_h2s, s_h2r.at[chunk, z], zz * 4 + y, tt
+            ).start()
+            return carry
+
+        pltpu.make_async_copy(h2.at[pl.ds(7 * t + q0, n)], h_place(z, t, chunk), s_h2r.at[chunk, z]).start()
+        lax.fori_loop(1, 64, send_h2, 0)
+
+    push_h(0)
+
+    def forward_d3(k, carry):
+        block = d2_block(4 - k)
+        await_bytes(block, s_d2r.at[k])
+        remote(block, block, s_d3s, s_d3r, d, sibling).start()
+        return carry
+
+    lax.fori_loop(1, 4, forward_d3, 0)
+    push_h(1)
+
+    await_bytes(dyb.at[:, :, 0:64, :], s_d3r)
 
     def product_g(which, g):
         total = dot(dyb[which, :, :, :512].reshape(512, 512), qb[0, g], 1, 1)
@@ -272,7 +294,29 @@
         gsum[1, g] = ours[:, 128:]
         return carry
 
-    lax.fori_loop(0, 7, grad_group, 0)
+    lax.fori_loop(0, 4, grad_group, 0)
+
+    def h_block(which, zz, chunk):
+        q0, n = CHUNKS[chunk]
+        return hb.at[which, :, q0 : q0 + n, pl.ds(pl.multiple_of(zz * 128, 128), 128), :]
+
+    def h_pass(k, chunk, which):
+        zz = lax.rem(z + k, 4)
+        return remote(
+            h_block(yi, zz, chunk), h_block(which, zz, chunk), s_hxs.at[chunk, k], s_hxr.at[chunk, k], d_t, t
+        )
+
+    def forward_h(chunk):
+        def step(k, carry):
+            zz = lax.rem(z + k, 4)
+            await_bytes(h_block(yi, zz, chunk), s_h2r.at[chunk, zz])
+            h_pass(k, chunk, yi).start()
+            return carry
+
+        lax.fori_loop(0, 4, step, 0)
+
+    forward_h(0)
+    lax.fori_loop(4, 7, grad_group, 0)
 
     def add_group(g, carry):
         remote(gsend.at[g], gx.at[g], s_gxs.at[g], s_gxr.at[g], d_t, t).wait_recv()
@@ -301,23 +345,7 @@
     pltpu.make_async_copy(g_piece(z, t), g_place(z, t), s_grr).start()
     lax.fori_loop(1, 64, send_gr, 0)
 
-    def h_block(which, zz):
-        return hb.at[which, :, :, pl.ds(pl.multiple_of(zz * 128, 128), 128), :]
-
-    def forward_h(k, carry):
-        zz = lax.rem(z + k, 4)
-        await_bytes(h_block(yi, zz), s_h2r.at[zz])
-        remote(h_block(yi, zz), h_block(yi, zz), s_hxs.at[k], s_hxr.at[k], d_t, t).start()
-        return carry
-
-    lax.fori_loop(0, 4, forward_h, 0)
-
-    def receive_h(k, carry):
-        zz = lax.rem(z + k, 4)
-        remote(h_block(yi, zz), h_block(yo, zz), s_hxs.at[k], s_hxr.at[k], d_t, t).wait_recv()
-        return carry
-
-    lax.fori_loop(0, 4, receive_h, 0)
+    forward_h(1)
 
     def product_d(q, half, c):
         cols = pl.ds(pl.multiple_of(c * 512, 512), 512)
@@ -332,7 +360,14 @@
             wg_ref[pl.ds(pl.multiple_of(q * 256 + 128 * half, 128), 128), :] = product_d(q, half, di)
         return carry
 
-    lax.fori_loop(0, 7, weight_group, 0)
+    for chunk, (q0, n) in enumerate(CHUNKS):
+
+        def receive_h(k, carry, chunk=chunk):
+            h_pass(k, chunk, yo).wait_recv()
+            return carry
+
+        lax.fori_loop(0, 4, receive_h, 0)
+        lax.fori_loop(q0, q0 + n, weight_group, 0)
 
     await_bytes(gr, s_grr)
 
@@ -363,76 +398,94 @@
 
     pltpu.make_async_copy(gm.at[pl.ds(7 * t, 7)], f_place(t), s_fr).start()
     lax.fori_loop(1, 16, send_f, 0)
+    def weight_finish(q, carry):
+        remote(dsend.at[q], dx.at[q], s_xs.at[q], s_xr.at[q], d_c, t).wait_recv()
+
+        def chunk(i, acc):
+            rows = rows16(q * 16 + i)
+            total = wg_ref[rows, :] + dx[q, rows16(i), :].astype(F32)
+            wg_ref[rows, :] = total * slopes[rows, :]
+            return acc + total * extra[rows, :]
+
+        acc = lax.fori_loop(0, 16, chunk, jnp.zeros((16, 512), F32))
+        sg_ref[pl.ds(q, 1), :] = jnp.sum(acc, axis=0, keepdims=True) * (1.0 / math.sqrt(1792.0))
+        return carry
+
+    lax.fori_loop(0, 7, weight_finish, 0)
     await_bytes(fr, s_fr)
 
+    await_bytes(h1.at[0:105], s_h1s)
+    await_bytes(gr.at[0:441], s_h2s)
+    await_bytes(gr.at[0:441], s_grs)
+    await_bytes(gm.at[0:105], s_fs)
+    await_bytes(dyb.at[0, 0, 0:112, :], s_d1s)
+    await_bytes(dyb.at[:, :, 0:48, :], s_d2s)
+    await_bytes(dyb.at[:, :, 0:64, :], s_d3s)
+
+    def drain7(g, carry):
+        remote(qb.at[di, g], qb.at[di, g], s_qs.at[g], s_qr.at[g], d_c, t).wait_send()
+        remote(gsend.at[g], gx.at[g], s_gxs.at[g], s_gxr.at[g], d_t, t).wait_send()
+        remote(dsend.at[g], dx.at[g], s_xs.at[g], s_xr.at[g], d_c, t).wait_send()
+        return carry
+
+    lax.fori_loop(0, 7, drain7, 0)
+
+    def drain4(k, carry):
+        for chunk in range(2):
+            h_pass(k, chunk, yi).wait_send()
+        return carry
+
+    lax.fori_loop(0, 4, drain4, 0)
+
+
+def finish_kernel(
+    gate_in, up_in, h256_in, fr_in, wg_in, sg_in, dgate_ref, dup_ref, wg_out, sg_out, gate, up, h256, fr, wg, sg, gh, sem
+):
+    bring = [
+        pltpu.make_async_copy(src, dst, sem.at[i])
+        for i, (src, dst) in enumerate(
+            ((wg_in, wg), (fr_in, fr), (h256_in, h256), (gate_in, gate), (up_in, up), (sg_in, sg))
+        )
+    ]
+    for copy in bring:
+        copy.start()
+    for copy in bring[1:]:
+        copy.wait()
+    sg_out[...] = sg[...]
+    bring[0].wait()
+    move = pltpu.make_async_copy(wg, wg_out, sem.at[0])
+    move.start()
     for q in range(7):
-        gh[...] = dot(fr[0, q], h256_ref[:128, :], 1, 0) + dot(fr[1, q], h256_ref[128:, :], 1, 0)
+        gh[...] = dot(fr[0, q], h256[:128, :], 1, 0) + dot(fr[1, q], h256[128:, :], 1, 0)
         cols = slice(256 * q, 256 * q + 256)
 
-        def finish(i, carry, cols=cols):
-            rows = rows16(i)
-            g = gate_ref[rows, cols].astype(F32)
-            u = up_ref[rows, cols].astype(F32)
+        def step(i, carry, cols=cols):
+            rows = pl.ds(pl.multiple_of(i * 16, 16), 16)
+            g = gate[rows, cols].astype(F32)
+            u = up[rows, cols].astype(F32)
             sig = jax.nn.sigmoid(g)
             grad = gh[rows, :] * sig
             dup_ref[rows, cols] = (grad * g).astype(BF16)
             dgate_ref[rows, cols] = (grad * u * (1.0 + g * (1.0 - sig))).astype(BF16)
             return carry
 
-        lax.fori_loop(0, 8, finish, 0)
-
-    def weight_finish(q, carry):
-        remote(dsend.at[q], dx.at[q], s_xs.at[q], s_xr.at[q], d_c, t).wait_recv()
-
-        def chunk(i, acc):
-            rows = rows16(q * 16 + i)
-            total = wg_ref[rows, :] + dx[q, rows16(i), :].astype(F32)
-            wg_ref[rows, :] = total * slopes[rows, :]
-            return acc + total * extra[rows, :]
-
-        acc = lax.fori_loop(0, 16, chunk, jnp.zeros((16, 512), F32))
-        sg_ref[pl.ds(q, 1), :] = jnp.sum(acc, axis=0, keepdims=True) * (1.0 / math.sqrt(1792.0))
-        return carry
-
-    lax.fori_loop(0, 7, weight_finish, 0)
-
-    await_bytes(h1.at[0:105], s_h1s)
-    await_bytes(gr.at[0:441], s_h2s)
-    await_bytes(gr.at[0:441], s_grs)
-    await_bytes(gm.at[0:105], s_fs)
-    await_bytes(dyb.at[0, 0, 0:112, :], s_d1s)
-    await_bytes(dyb.at[:, :, 0:112, :], s_d2s)
-
-    def drain7(g, carry):
-        remote(qb.at[di, g], qb.at[di, g], s_qs.at[g], s_qr.at[g], d_c, t).wait_send()
-        remote(gsend.at[g], gx.at[g], s_gxs.at[g], s_gxr.at[g], d_t, t).wait_send()
-        remote(dsend.at[g], dx.at[g], s_xs.at[g], s_xr.at[g], d_c, t).wait_send()
-        return carry
-
-    lax.fori_loop(0, 7, drain7, 0)
-
-    def drain4(k, carry):
-        zz = lax.rem(z + k, 4)
-        remote(h_block(yi, zz), h_block(yi, zz), s_hxs.at[k], s_hxr.at[k], d_t, t).wait_send()
-        return carry
-
-    lax.fori_loop(0, 4, drain4, 0)
+        lax.fori_loop(0, 8, step, 0)
+    move.wait()
 
 
 def shards(d_out, gate_pre, up_pre, down_weight, step_size):
     h256 = jnp.asarray(sylvester(256), BF16)
     vmem = pl.BlockSpec(memory_space=pltpu.VMEM)
     dma = pltpu.SemaphoreType.DMA
-    return pl.pallas_call(
+    fr, weight, step = pl.pallas_call(
         kernel,
         out_shape=(
-            jax.ShapeDtypeStruct((128, 1792), BF16),
-            jax.ShapeDtypeStruct((128, 1792), BF16),
+            jax.ShapeDtypeStruct((2, 7, 128, 128), BF16),
             jax.ShapeDtypeStruct((1792, 512), F32),
             jax.ShapeDtypeStruct((7, 512), F32),
         ),
         in_specs=[pl.BlockSpec(memory_space=pl.ANY)] + [vmem] * 5,
-        out_specs=(vmem,) * 4,
+        out_specs=(vmem,) * 3,
         scratch_shapes=[
             pltpu.VMEM((128, 1792), BF16),
             pltpu.VMEM((2, 7, 128, 128), BF16),
@@ -449,15 +502,13 @@
             pltpu.VMEM((2, 7, 512, 128), BF16),
             pltpu.VMEM((448, 16, 128), BF16),
             pltpu.VMEM((112, 16, 128), BF16),
-            pltpu.VMEM((2, 7, 128, 128), BF16),
-            pltpu.VMEM((128, 256), F32),
             pltpu.VMEM((7, 256, 512), BF16),
             pltpu.VMEM((7, 256, 512), BF16),
-            dma,
+            dma, dma,
+            dma, dma((2, 4)),
+            dma((2, 4)), dma((2, 4)),
             dma, dma,
             dma, dma((4,)),
-            dma((4,)), dma((4,)),
-            dma, dma,
             dma, dma,
             dma((7,)), dma((7,)),
             dma((7,)), dma((7,)),
@@ -470,6 +521,30 @@
         ),
         cost_estimate=pl.CostEstimate(flops=8_000_000_000, bytes_accessed=12_000_000, transcendentals=1_000_000),
     )(d_out, gate_pre, up_pre, down_weight, step_size, h256)
+    anywhere = pl.BlockSpec(memory_space=pl.ANY)
+    return pl.pallas_call(
+        finish_kernel,
+        out_shape=(
+            jax.ShapeDtypeStruct((128, 1792), BF16),
+            jax.ShapeDtypeStruct((128, 1792), BF16),
+            jax.ShapeDtypeStruct((1792, 512), F32),
+            jax.ShapeDtypeStruct((7, 512), F32),
+        ),
+        in_specs=[anywhere] * 6,
+        out_specs=(vmem, vmem, anywhere, vmem),
+        scratch_shapes=[
+            pltpu.VMEM((128, 1792), BF16),
+            pltpu.VMEM((128, 1792), BF16),
+            pltpu.VMEM((256, 256), BF16),
+            pltpu.VMEM((2, 7, 128, 128), BF16),
+            pltpu.VMEM((1792, 512), F32),
+            pltpu.VMEM((7, 512), F32),
+            pltpu.VMEM((128, 256), F32),
+            dma((6,)),
+        ],
+        compiler_params=pltpu.CompilerParams(vmem_limit_bytes=60 * 1024 * 1024),
+        cost_estimate=pl.CostEstimate(flops=200_000_000, bytes_accessed=10_000_000, transcendentals=300_000),
+    )(gate_pre, up_pre, h256, fr, weight, step)
 
 
 def solution(mesh):

time: 200 us -> 180 us (0.900)
  the two profiles are of different devices: /device:TPU:69 before, /device:TPU:31 now
where the time goes in v2:
time: 180 us
  Pallas kernels  179 us (99%)
    pallas_call x1, Pallas kernels, shards(): pl.pallas_call(kernel, out_shape=(jax.ShapeDtypeStruct((2, 7, 128, 128),...  174 us
    pallas_call x1, Pallas kernels, shards(): pl.pallas_call(finish_kernel, out_shape=(jax.ShapeDtypeStruct((128, 1792)...  5.69 us

profile of v2, /device:TPU:31, one launch (start us, length us, event | category | flops | bytes accessed | tf_op | source)
XLA Modules:
  0.0 180.1 jit_solution(14983663557555132190)
XLA Ops:
  0.6 173.8 %shard_map.93 = (bf16[2,7,128,128]{3,2,1,0:T(8,128)(2,1)}, f32[1792,512]{1,0:T(8,128)}, f32[7,512]{1,0:T(8,128)}) custom-call(bf16[128,8192]{1,0:T(8,128)(2,1)} %dy_ref.1, bf16[128,1792]{1,0:T(8,128)(2,1)} %gate_in.1, bf16[128,1792]{1,0:T(8,128)(2,1)} %up_in.1, bf16[1792,512]{1,0:T(8,128)(2,1)} %dw_ref.1, f32[7,512]{1,0:T(8,128)} %step_ref.1, ...), custom_call_target="tpu_custom_call" | custom-call | flops 8000000000 | bytes 12000000 | tf_op jit(solution)/shard_map/pallas_call | solution.py:480
  174.4 5.7 %shard_map.94 = (bf16[128,1792]{1,0:T(8,128)(2,1)}, bf16[128,1792]{1,0:T(8,128)(2,1)}, f32[1792,512]{1,0:T(8,128)}, f32[7,512]{1,0:T(8,128)}) custom-call(bf16[128,1792]{1,0:T(8,128)(2,1)} %gate_in.1, bf16[128,1792]{1,0:T(8,128)(2,1)} %up_in.1, bf16[256,256]{1,0:T(8,128)(2,1)} %constant.2.clone.h256_ref.h256_in, ...), custom_call_target="tpu_custom_call" | custom-call | flops 200000000 | bytes 10000000 | tf_op jit(solution)/shard_map/pallas_call | solution.py:525

commit v3 on v2

--- a/solution.py
+++ b/solution.py
@@ -249,24 +249,16 @@
     lax.fori_loop(0, 28, spread_h, 0)
     mix_paley(paley, mixf, h2, SCALE)
 
-    def h_place(zz, ti, chunk):
-        q0, n = CHUNKS[chunk]
-        return hb.at[yi, ti % 2, q0 : q0 + n, pl.ds(pl.multiple_of(zz * 128 + (ti // 2) * 16, 16), 16), :]
-
-    def push_h(chunk):
-        q0, n = CHUNKS[chunk]
-
-        def send_h2(j, carry):
-            zz, tt = peer64(j)
-            remote(
-                h2.at[pl.ds(7 * tt + q0, n)], h_place(z, t, chunk), s_h2s, s_h2r.at[chunk, z], zz * 4 + y, tt
-            ).start()
-            return carry
-
-        pltpu.make_async_copy(h2.at[pl.ds(7 * t + q0, n)], h_place(z, t, chunk), s_h2r.at[chunk, z]).start()
-        lax.fori_loop(1, 64, send_h2, 0)
-
-    push_h(0)
+    def h_place(zz, ti):
+        return hb.at[yi, ti % 2, :, pl.ds(pl.multiple_of(zz * 128 + (ti // 2) * 16, 16), 16), :]
+
+    def send_h2(j, carry):
+        zz, tt = peer64(j)
+        remote(h2.at[pl.ds(7 * tt, 7)], h_place(z, t), s_h2s, s_h2r, zz * 4 + y, tt).start()
+        return carry
+
+    pltpu.make_async_copy(h2.at[pl.ds(7 * t, 7)], h_place(z, t), s_h2r).start()
+    lax.fori_loop(1, 64, send_h2, 0)
 
     def forward_d3(k, carry):
         block = d2_block(4 - k)
@@ -275,7 +267,6 @@
         return carry
 
     lax.fori_loop(1, 4, forward_d3, 0)
-    push_h(1)
 
     await_bytes(dyb.at[:, :, 0:64, :], s_d3r)
 
@@ -294,29 +285,7 @@
         gsum[1, g] = ours[:, 128:]
         return carry
 
-    lax.fori_loop(0, 4, grad_group, 0)
-
-    def h_block(which, zz, chunk):
-        q0, n = CHUNKS[chunk]
-        return hb.at[which, :, q0 : q0 + n, pl.ds(pl.multiple_of(zz * 128, 128), 128), :]
-
-    def h_pass(k, chunk, which):
-        zz = lax.rem(z + k, 4)
-        return remote(
-            h_block(yi, zz, chunk), h_block(which, zz, chunk), s_hxs.at[chunk, k], s_hxr.at[chunk, k], d_t, t
-        )
-
-    def forward_h(chunk):
-        def step(k, carry):
-            zz = lax.rem(z + k, 4)
-            await_bytes(h_block(yi, zz, chunk), s_h2r.at[chunk, zz])
-            h_pass(k, chunk, yi).start()
-            return carry
-
-        lax.fori_loop(0, 4, step, 0)
-
-    forward_h(0)
-    lax.fori_loop(4, 7, grad_group, 0)
+    lax.fori_loop(0, 7, grad_group, 0)
 
     def add_group(g, carry):
         remote(gsend.at[g], gx.at[g], s_gxs.at[g], s_gxr.at[g], d_t, t).wait_recv()
@@ -329,23 +298,35 @@
 
         return lax.fori_loop(0, 8, chunk, carry)
 
-    lax.fori_loop(0, 7, add_group, 0)
-
-    def g_piece(zz, ti):
-        return gsum.at[ti % 2, :, pl.ds(pl.multiple_of(zz * 128 + (ti // 2) * 16, 16), 16), :]
-
-    def g_place(zz, ti):
-        return gr.at[pl.ds(zz * 112 + 7 * ti, 7)]
-
-    def send_gr(j, carry):
-        zz, tt = peer64(j)
-        remote(g_piece(zz, tt), g_place(z, t), s_grs, s_grr, zz * 4 + y, tt).start()
-        return carry
-
-    pltpu.make_async_copy(g_piece(z, t), g_place(z, t), s_grr).start()
-    lax.fori_loop(1, 64, send_gr, 0)
-
-    forward_h(1)
+    def push_g(chunk):
+        q0, n = CHUNKS[chunk]
+
+        def piece(zz, ti):
+            return gsum.at[ti % 2, q0 : q0 + n, pl.ds(pl.multiple_of(zz * 128 + (ti // 2) * 16, 16), 16), :]
+
+        place = gr.at[pl.ds(z * 112 + 7 * t + q0, n)]
+
+        def send_gr(j, carry):
+            zz, tt = peer64(j)
+            remote(piece(zz, tt), place, s_grs, s_grr, zz * 4 + y, tt).start()
+            return carry
+
+        lax.fori_loop(q0, q0 + n, add_group, 0)
+        pltpu.make_async_copy(piece(z, t), place, s_grr).start()
+        lax.fori_loop(1, 64, send_gr, 0)
+
+    push_g(0)
+
+    def h_pass(q, which):
+        return remote(hb.at[yi, :, q], hb.at[which, :, q], s_hxs.at[q], s_hxr.at[q], d_t, t)
+
+    def forward_h(q, carry):
+        h_pass(q, yi).start()
+        return carry
+
+    await_bytes(hb.at[yi], s_h2r)
+    lax.fori_loop(0, 7, forward_h, 0)
+    push_g(1)
 
     def product_d(q, half, c):
         cols = pl.ds(pl.multiple_of(c * 512, 512), 512)
@@ -353,6 +334,7 @@
         return total + dot(hb[1, half, q], dyb[1, :, :, cols].reshape(512, 512), 0, 0)
 
     def weight_group(q, carry):
+        h_pass(q, yo).wait_recv()
         for half in range(2):
             dsend[q, 128 * half : 128 * half + 128, :] = product_d(q, half, do).astype(BF16)
         remote(dsend.at[q], dx.at[q], s_xs.at[q], s_xr.at[q], d_c, t).start()
@@ -360,14 +342,7 @@
             wg_ref[pl.ds(pl.multiple_of(q * 256 + 128 * half, 128), 128), :] = product_d(q, half, di)
         return carry
 
-    for chunk, (q0, n) in enumerate(CHUNKS):
-
-        def receive_h(k, carry, chunk=chunk):
-            h_pass(k, chunk, yo).wait_recv()
-            return carry
-
-        lax.fori_loop(0, 4, receive_h, 0)
-        lax.fori_loop(q0, q0 + n, weight_group, 0)
+    lax.fori_loop(0, 7, weight_group, 0)
 
     await_bytes(gr, s_grr)
 
@@ -426,16 +401,10 @@
         remote(qb.at[di, g], qb.at[di, g], s_qs.at[g], s_qr.at[g], d_c, t).wait_send()
         remote(gsend.at[g], gx.at[g], s_gxs.at[g], s_gxr.at[g], d_t, t).wait_send()
         remote(dsend.at[g], dx.at[g], s_xs.at[g], s_xr.at[g], d_c, t).wait_send()
+        h_pass(g, yi).wait_send()
         return carry
 
     lax.fori_loop(0, 7, drain7, 0)
-
-    def drain4(k, carry):
-        for chunk in range(2):
-            h_pass(k, chunk, yi).wait_send()
-        return carry
-
-    lax.fori_loop(0, 4, drain4, 0)
 
 
 def finish_kernel(
@@ -505,8 +474,8 @@
             pltpu.VMEM((7, 256, 512), BF16),
             pltpu.VMEM((7, 256, 512), BF16),
             dma, dma,
-            dma, dma((2, 4)),
-            dma((2, 4)), dma((2, 4)),
+            dma, dma,
+            dma((7,)), dma((7,)),
             dma, dma,
             dma, dma((4,)),
             dma, dma,

time: 180 us -> 162 us (0.900)
  the two profiles are of different devices: /device:TPU:31 before, /device:TPU:32 now
where the time goes in v3:
time: 162 us; the launch traced here: 161 us
  Pallas kernels  160 us (99%)
    pallas_call x1, Pallas kernels, shards(): pl.pallas_call(kernel, out_shape=(jax.ShapeDtypeStruct((2, 7, 128, 128),...  154 us
    pallas_call x1, Pallas kernels, shards(): pl.pallas_call(finish_kernel, out_shape=(jax.ShapeDtypeStruct((128, 1792)...  5.69 us

profile of v3, /device:TPU:32, one launch (start us, length us, event | category | flops | bytes accessed | tf_op | source)
XLA Modules:
  0.0 160.8 jit_solution(11321210739973589656)
XLA Ops:
  0.6 154.4 %shard_map.93 = (bf16[2,7,128,128]{3,2,1,0:T(8,128)(2,1)}, f32[1792,512]{1,0:T(8,128)}, f32[7,512]{1,0:T(8,128)}) custom-call(bf16[128,8192]{1,0:T(8,128)(2,1)} %dy_ref.1, bf16[128,1792]{1,0:T(8,128)(2,1)} %gate_in.1, bf16[128,1792]{1,0:T(8,128)(2,1)} %up_in.1, bf16[1792,512]{1,0:T(8,128)(2,1)} %dw_ref.1, f32[7,512]{1,0:T(8,128)} %step_ref.1, ...), custom_call_target="tpu_custom_call" | custom-call | flops 8000000000 | bytes 12000000 | tf_op jit(solution)/shard_map/pallas_call | solution.py:449
  155.1 5.7 %shard_map.94 = (bf16[128,1792]{1,0:T(8,128)(2,1)}, bf16[128,1792]{1,0:T(8,128)(2,1)}, f32[1792,512]{1,0:T(8,128)}, f32[7,512]{1,0:T(8,128)}) custom-call(bf16[128,1792]{1,0:T(8,128)(2,1)} %gate_in.1, bf16[128,1792]{1,0:T(8,128)(2,1)} %up_in.1, bf16[256,256]{1,0:T(8,128)(2,1)} %constant.2.clone.h256_ref.h256_in, ...), custom_call_target="tpu_custom_call" | custom-call | flops 200000000 | bytes 10000000 | tf_op jit(solution)/shard_map/pallas_call | solution.py:494

commit v4 on v3

--- a/solution.py
+++ b/solution.py
@@ -170,22 +170,29 @@
         low = yy - (yy // 2) * (2 * yy - 3)
         return pl.ds(pl.multiple_of(512 * (zz * 4 + low + c * (3 - 2 * low)), 512), 512)
 
-    def send_d1(j, carry):
-        zz = lax.rem(z + j // 2, 4)
-        yy = y - yi + lax.rem(yi + j % 2, 2)
-        for c in range(2):
-            remote(
-                dy_ref.at[rows16(part), columns(zz, yy, c)],
-                dyb.at[yi, z, rows16(part), pl.ds(512 * c, 512)],
-                s_d1s, s_d1r, zz * 4 + yy, t,
-            ).start()
-        return carry
-
+    def send_d1(other):
+        yy = y - yi + (yo if other else yi)
+
+        def step(j, carry):
+            zz = lax.rem(z + j, 4)
+            for c in range(2):
+                remote(
+                    dy_ref.at[rows16(part), columns(zz, yy, c)],
+                    dyb.at[yi, z, rows16(part), pl.ds(512 * c, 512)],
+                    s_d1s, s_d1r.at[other], zz * 4 + yy, t,
+                ).start()
+            return carry
+
+        lax.fori_loop(1 - other, 4, step, 0)
+
+    send_d1(1)
     for c in range(2):
         pltpu.make_async_copy(
-            dy_ref.at[rows16(part), columns(z, y, c)], dyb.at[yi, z, rows16(part), pl.ds(512 * c, 512)], s_d1r
+            dy_ref.at[rows16(part), columns(z, y, c)],
+            dyb.at[yi, z, rows16(part), pl.ds(512 * c, 512)],
+            s_d1r.at[0],
         ).start()
-    lax.fori_loop(1, 8, send_d1, 0)
+    send_d1(0)
 
     def send_h1(k, carry):
         p = lax.rem(t + k, 16)
@@ -220,20 +227,34 @@
 
     lax.fori_loop(0, 7, quant_group, 0)
 
-    await_bytes(dyb.at[0, :, 0:32, :], s_d1r)
-
     sibling = t + 1 - 2 * lh
 
-    def d2_block(k):
-        return dyb.at[:, :, rows16(lax.rem(part + 2 * k, 8)), :]
-
-    def send_d2(k, carry):
-        p = hi8 + lax.rem(part + 2 * k, 8)
-        remote(d2_block(0), d2_block(0), s_d2s, s_d2r.at[k], d, p).start()
-        return carry
-
-    lax.fori_loop(1, 4, send_d2, 0)
-    remote(d2_block(0), d2_block(0), s_d3s, s_d3r, d, sibling).start()
+    def d2_block(other, k):
+        return dyb.at[yo if other else yi, :, rows16(lax.rem(part + 2 * k, 8)), :]
+
+    def push_d2(other):
+        await_bytes(dyb.at[0, :, 0:16, :], s_d1r.at[other])
+        block = d2_block(other, 0)
+
+        def send_d2(k, carry):
+            remote(block, block, s_d2s, s_d2r.at[other, k], d, hi8 + lax.rem(part + 2 * k, 8)).start()
+            return carry
+
+        lax.fori_loop(1, 4, send_d2, 0)
+        remote(block, block, s_d3s, s_d3r.at[other], d, sibling).start()
+
+    def push_d3(other):
+        def forward_d3(k, carry):
+            block = d2_block(other, 4 - k)
+            await_bytes(block, s_d2r.at[other, k])
+            remote(block, block, s_d3s, s_d3r.at[other], d, sibling).start()
+            return carry
+
+        lax.fori_loop(1, 4, forward_d3, 0)
+
+    push_d2(1)
+    push_d2(0)
+    push_d3(1)
 
     await_bytes(h1, s_h1r)
 
@@ -260,15 +281,8 @@
     pltpu.make_async_copy(h2.at[pl.ds(7 * t, 7)], h_place(z, t), s_h2r).start()
     lax.fori_loop(1, 64, send_h2, 0)
 
-    def forward_d3(k, carry):
-        block = d2_block(4 - k)
-        await_bytes(block, s_d2r.at[k])
-        remote(block, block, s_d3s, s_d3r, d, sibling).start()
-        return carry
-
-    lax.fori_loop(1, 4, forward_d3, 0)
-
-    await_bytes(dyb.at[:, :, 0:64, :], s_d3r)
+    push_d3(0)
+    await_bytes(dyb.at[0, :, 0:64, :], s_d3r.at[1])
 
     def product_g(which, g):
         total = dot(dyb[which, :, :, :512].reshape(512, 512), qb[0, g], 1, 1)
@@ -280,12 +294,18 @@
         gsend[g, 0] = theirs[:, :128]
         gsend[g, 1] = theirs[:, 128:]
         remote(gsend.at[g], gx.at[g], s_gxs.at[g], s_gxr.at[g], d_t, t).start()
+        return carry
+
+    lax.fori_loop(0, 7, grad_group, 0)
+    await_bytes(dyb.at[0, :, 0:64, :], s_d3r.at[0])
+
+    def own_group(g, carry):
         ours = product_g(yi, g).astype(BF16)
         gsum[0, g] = ours[:, :128]
         gsum[1, g] = ours[:, 128:]
         return carry
 
-    lax.fori_loop(0, 7, grad_group, 0)
+    lax.fori_loop(0, 7, own_group, 0)
 
     def add_group(g, carry):
         remote(gsend.at[g], gx.at[g], s_gxs.at[g], s_gxr.at[g], d_t, t).wait_recv()
@@ -476,9 +496,9 @@
             dma, dma,
             dma, dma,
             dma((7,)), dma((7,)),
-            dma, dma,
-            dma, dma((4,)),
-            dma, dma,
+            dma, dma((2,)),
+            dma, dma((2, 4)),
+            dma, dma((2,)),
             dma((7,)), dma((7,)),
             dma((7,)), dma((7,)),
             dma, dma,

time: 162 us -> 148 us (0.914)
  the two profiles are of different devices: /device:TPU:32 before, /device:TPU:39 now
where the time goes in v4:
time: 148 us; the launch traced here: 147 us
  Pallas kernels  147 us (99%)
    pallas_call x1, Pallas kernels, shards(): pl.pallas_call(kernel, out_shape=(jax.ShapeDtypeStruct((2, 7, 128, 128),...  141 us
    pallas_call x1, Pallas kernels, shards(): pl.pallas_call(finish_kernel, out_shape=(jax.ShapeDtypeStruct((128, 1792)...  5.69 us

profile of v4, /device:TPU:39, one launch (start us, length us, event | category | flops | bytes accessed | tf_op | source)
XLA Modules:
  0.0 147.4 jit_solution(14490246158321005461)
XLA Ops:
  0.6 141.1 %shard_map.93 = (bf16[2,7,128,128]{3,2,1,0:T(8,128)(2,1)}, f32[1792,512]{1,0:T(8,128)}, f32[7,512]{1,0:T(8,128)}) custom-call(bf16[128,8192]{1,0:T(8,128)(2,1)} %dy_ref.1, bf16[128,1792]{1,0:T(8,128)(2,1)} %gate_in.1, bf16[128,1792]{1,0:T(8,128)(2,1)} %up_in.1, bf16[1792,512]{1,0:T(8,128)(2,1)} %dw_ref.1, f32[7,512]{1,0:T(8,128)} %step_ref.1, ...), custom_call_target="tpu_custom_call" | custom-call | flops 8000000000 | bytes 12000000 | tf_op jit(solution)/shard_map/pallas_call | solution.py:469
  141.8 5.7 %shard_map.94 = (bf16[128,1792]{1,0:T(8,128)(2,1)}, bf16[128,1792]{1,0:T(8,128)(2,1)}, f32[1792,512]{1,0:T(8,128)}, f32[7,512]{1,0:T(8,128)}) custom-call(bf16[128,1792]{1,0:T(8,128)(2,1)} %gate_in.1, bf16[128,1792]{1,0:T(8,128)(2,1)} %up_in.1, bf16[256,256]{1,0:T(8,128)(2,1)} %constant.2.clone.h256_ref.h256_in, ...), custom_call_target="tpu_custom_call" | custom-call | flops 200000000 | bytes 10000000 | tf_op jit(solution)/shard_map/pallas_call | solution.py:514

commit v5 on v4

--- a/solution.py
+++ b/solution.py
@@ -103,11 +103,11 @@
 
 
 def kernel(
-    dy_ref, gate_ref, up_ref, dw_ref, step_ref, h256_ref,
-    fr, wg_ref, sg_ref,
-    hid, hs, h1, mixf, h2, hb, dyb, qb, slopes, extra, gsend, gx, gsum, gr, gm, dsend, dx,
+    dy_ref, gate_in, up_in, dw_in, step_ref, h256_ref,
+    dgate_out, dup_out, wg_out, sg_ref,
+    gate_ref, up_ref, dw_ref, dgate, dup, up_factor, gate_factor, fr, gh, wg_ref, hid, hs, h1, mixf, h2, hb, dyb, qb, slopes, extra, gsend, gx, gsum, gr, gm, dsend, dx,
     s_h1s, s_h1r, s_h2s, s_h2r, s_hxs, s_hxr, s_d1s, s_d1r, s_d2s, s_d2r, s_d3s, s_d3r, s_qs, s_qr,
-    s_gxs, s_gxr, s_grs, s_grr, s_fs, s_fr, s_xs, s_xr,
+    s_gxs, s_gxr, s_grs, s_grr, s_fs, s_fr, s_xs, s_xr, s_w, s_in, s_gate, s_up,
 ):
     paley = paley_matrix()
     sin_series, cos_series = half_turn_series()
@@ -149,20 +149,12 @@
         pl.semaphore_signal(barrier, inc=1, device_id=(zz * 4 + y + 1 - 2 * yi, t), device_id_type=MESH)
     pl.semaphore_signal(barrier, inc=1, device_id=(d_c, t), device_id_type=MESH)
 
-    def hidden_step(i, carry):
-        rows = rows16(i)
-        for q in range(7):
-            cols = slice(256 * q, 256 * q + 256)
-            g = gate_ref[rows, cols].astype(F32)
-            u = up_ref[rows, cols].astype(F32)
-            hid[rows, cols] = (g * jax.nn.sigmoid(g) * u).astype(BF16)
-        return carry
-
-    lax.fori_loop(0, 8, hidden_step, 0)
-    for q in range(7):
-        turned = dot(hid[:, 256 * q : 256 * q + 256], h256_ref[...], 1, 0).astype(BF16)
-        hs[0, q] = turned[:, :128]
-        hs[1, q] = turned[:, 128:]
+    fetch = [
+        pltpu.make_async_copy(src, dst, s_in.at[i])
+        for i, (src, dst) in enumerate(((gate_in, gate_ref), (up_in, up_ref), (dw_in, dw_ref)))
+    ]
+    for copy in fetch:
+        copy.start()
 
     pl.semaphore_wait(barrier, 68)
 
@@ -193,6 +185,24 @@
             s_d1r.at[0],
         ).start()
     send_d1(0)
+
+    fetch[0].wait()
+    fetch[1].wait()
+
+    def hidden_step(i, carry):
+        rows = rows16(i)
+        for q in range(7):
+            cols = slice(256 * q, 256 * q + 256)
+            g = gate_ref[rows, cols].astype(F32)
+            u = up_ref[rows, cols].astype(F32)
+            hid[rows, cols] = (g * jax.nn.sigmoid(g) * u).astype(BF16)
+        return carry
+
+    lax.fori_loop(0, 8, hidden_step, 0)
+    for q in range(7):
+        turned = dot(hid[:, 256 * q : 256 * q + 256], h256_ref[...], 1, 0).astype(BF16)
+        hs[0, q] = turned[:, :128]
+        hs[1, q] = turned[:, 128:]
 
     def send_h1(k, carry):
         p = lax.rem(t + k, 16)
@@ -225,6 +235,7 @@
         remote(qb.at[di, g], qb.at[di, g], s_qs.at[g], s_qr.at[g], d_c, t).start()
         return carry
 
+    fetch[2].wait()
     lax.fori_loop(0, 7, quant_group, 0)
 
     sibling = t + 1 - 2 * lh
@@ -307,6 +318,19 @@
 
     lax.fori_loop(0, 7, own_group, 0)
 
+    def factor_step(i, carry):
+        rows = rows16(i)
+        for q in range(7):
+            cols = slice(256 * q, 256 * q + 256)
+            g = gate_ref[rows, cols].astype(F32)
+            u = up_ref[rows, cols].astype(F32)
+            sig = jax.nn.sigmoid(g)
+            up_factor[rows, cols] = g * sig
+            gate_factor[rows, cols] = u * sig * (1.0 + g * (1.0 - sig))
+        return carry
+
+    lax.fori_loop(0, 8, factor_step, 0)
+
     def add_group(g, carry):
         remote(gsend.at[g], gx.at[g], s_gxs.at[g], s_gxr.at[g], d_t, t).wait_recv()
 
@@ -362,7 +386,7 @@
             wg_ref[pl.ds(pl.multiple_of(q * 256 + 128 * half, 128), 128), :] = product_d(q, half, di)
         return carry
 
-    lax.fori_loop(0, 7, weight_group, 0)
+    lax.fori_loop(0, 6, weight_group, 0)
 
     await_bytes(gr, s_grr)
 
@@ -393,6 +417,11 @@
 
     pltpu.make_async_copy(gm.at[pl.ds(7 * t, 7)], f_place(t), s_fr).start()
     lax.fori_loop(1, 16, send_f, 0)
+    lax.fori_loop(6, 7, weight_group, 0)
+    def leave_w(q):
+        rows = pl.ds(pl.multiple_of(q * 256, 256), 256)
+        return pltpu.make_async_copy(wg_ref.at[rows, :], wg_out.at[rows, :], s_w.at[q])
+
     def weight_finish(q, carry):
         remote(dsend.at[q], dx.at[q], s_xs.at[q], s_xr.at[q], d_c, t).wait_recv()
 
@@ -403,11 +432,29 @@
             return acc + total * extra[rows, :]
 
         acc = lax.fori_loop(0, 16, chunk, jnp.zeros((16, 512), F32))
+        leave_w(q).start()
         sg_ref[pl.ds(q, 1), :] = jnp.sum(acc, axis=0, keepdims=True) * (1.0 / math.sqrt(1792.0))
         return carry
 
     lax.fori_loop(0, 7, weight_finish, 0)
     await_bytes(fr, s_fr)
+    leave_g = []
+    for q in range(7):
+        gh[...] = dot(fr[0, q], h256_ref[:128, :], 1, 0) + dot(fr[1, q], h256_ref[128:, :], 1, 0)
+        cols = slice(256 * q, 256 * q + 256)
+
+        def finish_step(i, carry, cols=cols):
+            rows = rows16(i)
+            grad = gh[rows, :]
+            dup[rows, cols] = (grad * up_factor[rows, cols]).astype(BF16)
+            dgate[rows, cols] = (grad * gate_factor[rows, cols]).astype(BF16)
+            return carry
+
+        lax.fori_loop(0, 8, finish_step, 0, unroll=True)
+        leave_g.append(pltpu.make_async_copy(dgate.at[:, cols], dgate_out.at[:, cols], s_gate.at[q]))
+        leave_g.append(pltpu.make_async_copy(dup.at[:, cols], dup_out.at[:, cols], s_up.at[q]))
+        leave_g[-1].start()
+        leave_g[-2].start()
 
     await_bytes(h1.at[0:105], s_h1s)
     await_bytes(gr.at[0:441], s_h2s)
@@ -422,60 +469,56 @@
         remote(gsend.at[g], gx.at[g], s_gxs.at[g], s_gxr.at[g], d_t, t).wait_send()
         remote(dsend.at[g], dx.at[g], s_xs.at[g], s_xr.at[g], d_c, t).wait_send()
         h_pass(g, yi).wait_send()
+        leave_w(g).wait()
         return carry
 
     lax.fori_loop(0, 7, drain7, 0)
-
-
-def finish_kernel(
-    gate_in, up_in, h256_in, fr_in, wg_in, sg_in, dgate_ref, dup_ref, wg_out, sg_out, gate, up, h256, fr, wg, sg, gh, sem
-):
-    bring = [
-        pltpu.make_async_copy(src, dst, sem.at[i])
-        for i, (src, dst) in enumerate(
-            ((wg_in, wg), (fr_in, fr), (h256_in, h256), (gate_in, gate), (up_in, up), (sg_in, sg))
-        )
-    ]
+    for copy in leave_g:
+        copy.wait()
+
+
+def copy_kernel(dgate_in, dup_in, wg_in, sg_in, dgate_out, dup_out, wg_out, sg_out, dgate, dup, wg, sg, s_in, s_out):
+    routes = [(sg_in, sg, sg_out), (dgate_in, dgate, dgate_out), (dup_in, dup, dup_out)]
+    for q in range(7):
+        rows = pl.ds(256 * q, 256)
+        routes.append((wg_in.at[rows, :], wg.at[rows, :], wg_out.at[rows, :]))
+    bring = [pltpu.make_async_copy(src, via, s_in.at[i]) for i, (src, via, _) in enumerate(routes)]
+    leave = [pltpu.make_async_copy(via, dst, s_out.at[i]) for i, (_, via, dst) in enumerate(routes)]
     for copy in bring:
         copy.start()
-    for copy in bring[1:]:
+    for copy, then in zip(bring, leave):
         copy.wait()
-    sg_out[...] = sg[...]
-    bring[0].wait()
-    move = pltpu.make_async_copy(wg, wg_out, sem.at[0])
-    move.start()
-    for q in range(7):
-        gh[...] = dot(fr[0, q], h256[:128, :], 1, 0) + dot(fr[1, q], h256[128:, :], 1, 0)
-        cols = slice(256 * q, 256 * q + 256)
-
-        def step(i, carry, cols=cols):
-            rows = pl.ds(pl.multiple_of(i * 16, 16), 16)
-            g = gate[rows, cols].astype(F32)
-            u = up[rows, cols].astype(F32)
-            sig = jax.nn.sigmoid(g)
-            grad = gh[rows, :] * sig
-            dup_ref[rows, cols] = (grad * g).astype(BF16)
-            dgate_ref[rows, cols] = (grad * u * (1.0 + g * (1.0 - sig))).astype(BF16)
-            return carry
-
-        lax.fori_loop(0, 8, step, 0)
-    move.wait()
+        then.start()
+    for copy in leave:
+        copy.wait()
 
 
 def shards(d_out, gate_pre, up_pre, down_weight, step_size):
     h256 = jnp.asarray(sylvester(256), BF16)
     vmem = pl.BlockSpec(memory_space=pltpu.VMEM)
     dma = pltpu.SemaphoreType.DMA
-    fr, weight, step = pl.pallas_call(
+    anywhere = pl.BlockSpec(memory_space=pl.ANY)
+    results = pl.pallas_call(
         kernel,
         out_shape=(
-            jax.ShapeDtypeStruct((2, 7, 128, 128), BF16),
+            jax.ShapeDtypeStruct((128, 1792), BF16),
+            jax.ShapeDtypeStruct((128, 1792), BF16),
             jax.ShapeDtypeStruct((1792, 512), F32),
             jax.ShapeDtypeStruct((7, 512), F32),
         ),
-        in_specs=[pl.BlockSpec(memory_space=pl.ANY)] + [vmem] * 5,
-        out_specs=(vmem,) * 3,
+        in_specs=[anywhere] * 4 + [vmem] * 2,
+        out_specs=(anywhere, anywhere, anywhere, vmem),
         scratch_shapes=[
+            pltpu.VMEM((128, 1792), BF16),
+            pltpu.VMEM((128, 1792), BF16),
+            pltpu.VMEM((1792, 512), BF16),
+            pltpu.VMEM((128, 1792), BF16),
+            pltpu.VMEM((128, 1792), BF16),
+            pltpu.VMEM((128, 1792), F32),
+            pltpu.VMEM((128, 1792), F32),
+            pltpu.VMEM((2, 7, 128, 128), BF16),
+            pltpu.VMEM((128, 256), F32),
+            pltpu.VMEM((1792, 512), F32),
             pltpu.VMEM((128, 1792), BF16),
             pltpu.VMEM((2, 7, 128, 128), BF16),
             pltpu.VMEM((112, 16, 128), BF16),
@@ -504,36 +547,34 @@
             dma, dma,
             dma, dma,
             dma((7,)), dma((7,)),
+            dma((7,)),
+            dma((3,)), dma((7,)), dma((7,)),
         ],
         compiler_params=pltpu.CompilerParams(
             collective_id=0, has_side_effects=True, vmem_limit_bytes=58 * 1024 * 1024
         ),
         cost_estimate=pl.CostEstimate(flops=8_000_000_000, bytes_accessed=12_000_000, transcendentals=1_000_000),
     )(d_out, gate_pre, up_pre, down_weight, step_size, h256)
-    anywhere = pl.BlockSpec(memory_space=pl.ANY)
     return pl.pallas_call(
-        finish_kernel,
+        copy_kernel,
         out_shape=(
             jax.ShapeDtypeStruct((128, 1792), BF16),
             jax.ShapeDtypeStruct((128, 1792), BF16),
             jax.ShapeDtypeStruct((1792, 512), F32),
             jax.ShapeDtypeStruct((7, 512), F32),
         ),
-        in_specs=[anywhere] * 6,
-        out_specs=(vmem, vmem, anywhere, vmem),
+        in_specs=[anywhere] * 4,
+        out_specs=(anywhere,) * 4,
         scratch_shapes=[
             pltpu.VMEM((128, 1792), BF16),
             pltpu.VMEM((128, 1792), BF16),
-            pltpu.VMEM((256, 256), BF16),
-            pltpu.VMEM((2, 7, 128, 128), BF16),
             pltpu.VMEM((1792, 512), F32),
             pltpu.VMEM((7, 512), F32),
-            pltpu.VMEM((128, 256), F32),
-            dma((6,)),
+            dma((10,)), dma((10,)),
         ],
         compiler_params=pltpu.CompilerParams(vmem_limit_bytes=60 * 1024 * 1024),
-        cost_estimate=pl.CostEstimate(flops=200_000_000, bytes_accessed=10_000_000, transcendentals=300_000),
-    )(gate_pre, up_pre, h256, fr, weight, step)
+        cost_estimate=pl.CostEstimate(flops=0, bytes_accessed=10_000_000, transcendentals=0),
+    )(*results)
 
 
 def solution(mesh):

time: 148 us -> 140 us (0.946)
  the two profiles are of different devices: /device:TPU:39 before, /device:TPU:32 now
where the time goes in v5:
time: 140 us; the launch traced here: 139 us
  Pallas kernels  138 us (99%)
    pallas_call x1, Pallas kernels, shards(): pl.pallas_call(kernel, out_shape=(jax.ShapeDtypeStruct((128, 1792), BF16)...  134 us
    pallas_call x1, Pallas kernels, shards(): pl.pallas_call(copy_kernel, out_shape=(jax.ShapeDtypeStruct((128, 1792),...  4.13 us

profile of v5, /device:TPU:32, one launch (start us, length us, event | category | flops | bytes accessed | tf_op | source)
XLA Modules:
  0.0 138.9 jit_solution(1154370626674242492)
XLA Ops:
  0.6 134.1 %shard_map.93 = (bf16[128,1792]{1,0:T(8,128)(2,1)}, bf16[128,1792]{1,0:T(8,128)(2,1)}, f32[1792,512]{1,0:T(8,128)}, f32[7,512]{1,0:T(8,128)}) custom-call(bf16[128,8192]{1,0:T(8,128)(2,1)} %dy_ref.1, bf16[128,1792]{1,0:T(8,128)(2,1)} %gate_in.1, bf16[128,1792]{1,0:T(8,128)(2,1)} %up_in.1, bf16[1792,512]{1,0:T(8,128)(2,1)} %dw_in.1, f32[7,512]{1,0:T(8,128)} %step_ref.1, ...), custom_call_target="tpu_custom_call" | custom-call | flops 8000000000 | bytes 12000000 | tf_op jit(solution)/shard_map/pallas_call | solution.py:501
  134.7 4.1 %shard_map.94 = (bf16[128,1792]{1,0:T(8,128)(2,1)}, bf16[128,1792]{1,0:T(8,128)(2,1)}, f32[1792,512]{1,0:T(8,128)}, f32[7,512]{1,0:T(8,128)}) custom-call(bf16[128,1792]{1,0:T(8,128)(2,1)} %get-tuple-element.8.dgate_in, bf16[128,1792]{1,0:T(8,128)(2,1)} %get-tuple-element.9.dup_in, f32[1792,512]{1,0:T(8,128)} %get-tuple-element.10.wg_in, ...), custom_call_target="tpu_custom_call" | custom-call | bytes 10000000 | tf_op jit(solution)/shard_map/pallas_call | solution.py:558

commit v6 on v5

--- a/solution.py
+++ b/solution.py
@@ -103,9 +103,9 @@
 
 
 def kernel(
-    dy_ref, gate_in, up_in, dw_in, step_ref, h256_ref,
+    dy_ref, gate_in, up_in, dw_in, step_in, h256_in,
     dgate_out, dup_out, wg_out, sg_ref,
-    gate_ref, up_ref, dw_ref, dgate, dup, up_factor, gate_factor, fr, gh, wg_ref, hid, hs, h1, mixf, h2, hb, dyb, qb, slopes, extra, gsend, gx, gsum, gr, gm, dsend, dx,
+    gate_ref, up_ref, dw_ref, step_ref, h256_ref, dgate, dup, up_factor, gate_factor, fr, gh, wg_ref, hid, hs, h1, mixf, h2, hb, dyb, qb, slopes, extra, gsend, gx, gsum, gr, gm, dsend, dx,
     s_h1s, s_h1r, s_h2s, s_h2r, s_hxs, s_hxr, s_d1s, s_d1r, s_d2s, s_d2r, s_d3s, s_d3r, s_qs, s_qr,
     s_gxs, s_gxr, s_grs, s_grr, s_fs, s_fr, s_xs, s_xr, s_w, s_in, s_gate, s_up,
 ):
@@ -135,7 +135,7 @@
         return pl.ds(pl.multiple_of(i * 16, 16), 16)
 
     def peer64(j):
-        return lax.rem(z + j % 4, 4) , lax.rem(t + j // 4, 16)
+        return lax.rem(z + j % 4, 4) , lax.rem(t + 9 * (j // 4), 16)
 
     barrier = pltpu.get_barrier_semaphore()
 
@@ -151,7 +151,9 @@
 
     fetch = [
         pltpu.make_async_copy(src, dst, s_in.at[i])
-        for i, (src, dst) in enumerate(((gate_in, gate_ref), (up_in, up_ref), (dw_in, dw_ref)))
+        for i, (src, dst) in enumerate(
+            ((gate_in, gate_ref), (up_in, up_ref), (h256_in, h256_ref), (dw_in, dw_ref), (step_in, step_ref))
+        )
     ]
     for copy in fetch:
         copy.start()
@@ -186,8 +188,8 @@
         ).start()
     send_d1(0)
 
-    fetch[0].wait()
-    fetch[1].wait()
+    for copy in fetch[:3]:
+        copy.wait()
 
     def hidden_step(i, carry):
         rows = rows16(i)
@@ -205,7 +207,7 @@
         hs[1, q] = turned[:, 128:]
 
     def send_h1(k, carry):
-        p = lax.rem(t + k, 16)
+        p = lax.rem(t + 9 * k, 16)
         remote(hs.at[p % 2, :, rows16(p // 2), :], h1.at[pl.ds(7 * t, 7)], s_h1s, s_h1r, d, p).start()
         return carry
 
@@ -235,7 +237,8 @@
         remote(qb.at[di, g], qb.at[di, g], s_qs.at[g], s_qr.at[g], d_c, t).start()
         return carry
 
-    fetch[2].wait()
+    fetch[3].wait()
+    fetch[4].wait()
     lax.fori_loop(0, 7, quant_group, 0)
 
     sibling = t + 1 - 2 * lh
@@ -386,7 +389,7 @@
             wg_ref[pl.ds(pl.multiple_of(q * 256 + 128 * half, 128), 128), :] = product_d(q, half, di)
         return carry
 
-    lax.fori_loop(0, 6, weight_group, 0)
+    lax.fori_loop(0, 5, weight_group, 0)
 
     await_bytes(gr, s_grr)
 
@@ -411,13 +414,13 @@
         return fr.at[ti % 2, :, rows16(ti // 2), :]
 
     def send_f(k, carry):
-        p = lax.rem(t + k, 16)
+        p = lax.rem(t + 9 * k, 16)
         remote(gm.at[pl.ds(7 * p, 7)], f_place(t), s_fs, s_fr, d, p).start()
         return carry
 
     pltpu.make_async_copy(gm.at[pl.ds(7 * t, 7)], f_place(t), s_fr).start()
     lax.fori_loop(1, 16, send_f, 0)
-    lax.fori_loop(6, 7, weight_group, 0)
+    lax.fori_loop(5, 7, weight_group, 0)
     def leave_w(q):
         rows = pl.ds(pl.multiple_of(q * 256, 256), 256)
         return pltpu.make_async_copy(wg_ref.at[rows, :], wg_out.at[rows, :], s_w.at[q])
@@ -506,12 +509,14 @@
             jax.ShapeDtypeStruct((1792, 512), F32),
             jax.ShapeDtypeStruct((7, 512), F32),
         ),
-        in_specs=[anywhere] * 4 + [vmem] * 2,
+        in_specs=[anywhere] * 6,
         out_specs=(anywhere, anywhere, anywhere, vmem),
         scratch_shapes=[
             pltpu.VMEM((128, 1792), BF16),
             pltpu.VMEM((128, 1792), BF16),
             pltpu.VMEM((1792, 512), BF16),
+            pltpu.VMEM((7, 512), F32),
+            pltpu.VMEM((256, 256), BF16),
             pltpu.VMEM((128, 1792), BF16),
             pltpu.VMEM((128, 1792), BF16),
             pltpu.VMEM((128, 1792), F32),
@@ -548,7 +553,7 @@
             dma, dma,
             dma((7,)), dma((7,)),
             dma((7,)),
-            dma((3,)), dma((7,)), dma((7,)),
+            dma((5,)), dma((7,)), dma((7,)),
         ],
         compiler_params=pltpu.CompilerParams(
             collective_id=0, has_side_effects=True, vmem_limit_bytes=58 * 1024 * 1024

time: 140 us -> 140 us (level)
  no operation moved by 1% of the time
where the time goes in v6:
time: 140 us; the launch traced here: 139 us
  Pallas kernels  139 us (99%)
    pallas_call x1, Pallas kernels, shards(): pl.pallas_call(kernel, out_shape=(jax.ShapeDtypeStruct((128, 1792), BF16)...  135 us
    pallas_call x1, Pallas kernels, shards(): pl.pallas_call(copy_kernel, out_shape=(jax.ShapeDtypeStruct((128, 1792),...  4.13 us

profile of v6, /device:TPU:32, one launch (start us, length us, event | category | flops | bytes accessed | tf_op | source)
XLA Modules:
  0.0 139.5 jit_solution(5671042828548550524)
XLA Ops:
  0.6 134.7 %shard_map.93 = (bf16[128,1792]{1,0:T(8,128)(2,1)}, bf16[128,1792]{1,0:T(8,128)(2,1)}, f32[1792,512]{1,0:T(8,128)}, f32[7,512]{1,0:T(8,128)}) custom-call(bf16[128,8192]{1,0:T(8,128)(2,1)} %dy_ref.1, bf16[128,1792]{1,0:T(8,128)(2,1)} %gate_in.1, bf16[128,1792]{1,0:T(8,128)(2,1)} %up_in.1, bf16[1792,512]{1,0:T(8,128)(2,1)} %dw_in.1, f32[7,512]{1,0:T(8,128)} %step_in.1, ...), custom_call_target="tpu_custom_call" | custom-call | flops 8000000000 | bytes 12000000 | tf_op jit(solution)/shard_map/pallas_call | solution.py:504
  135.3 4.1 %shard_map.94 = (bf16[128,1792]{1,0:T(8,128)(2,1)}, bf16[128,1792]{1,0:T(8,128)(2,1)}, f32[1792,512]{1,0:T(8,128)}, f32[7,512]{1,0:T(8,128)}) custom-call(bf16[128,1792]{1,0:T(8,128)(2,1)} %get-tuple-element.8.dgate_in, bf16[128,1792]{1,0:T(8,128)(2,1)} %get-tuple-element.9.dup_in, f32[1792,512]{1,0:T(8,128)} %get-tuple-element.10.wg_in, ...), custom_call_target="tpu_custom_call" | custom-call | bytes 10000000 | tf_op jit(solution)/shard_map/pallas_call | solution.py:563

commit v7 on v6

--- a/solution.py
+++ b/solution.py
@@ -439,7 +439,7 @@
         sg_ref[pl.ds(q, 1), :] = jnp.sum(acc, axis=0, keepdims=True) * (1.0 / math.sqrt(1792.0))
         return carry
 
-    lax.fori_loop(0, 7, weight_finish, 0)
+    lax.fori_loop(0, 5, weight_finish, 0)
     await_bytes(fr, s_fr)
     leave_g = []
     for q in range(7):
@@ -458,6 +458,7 @@
         leave_g.append(pltpu.make_async_copy(dup.at[:, cols], dup_out.at[:, cols], s_up.at[q]))
         leave_g[-1].start()
         leave_g[-2].start()
+    lax.fori_loop(5, 7, weight_finish, 0)
 
     await_bytes(h1.at[0:105], s_h1s)
     await_bytes(gr.at[0:441], s_h2s)

time: 140 us -> 139 us (level)
  no operation moved by 1% of the time
where the time goes in v7:
time: 139 us
  Pallas kernels  138 us (99%)
    pallas_call x1, Pallas kernels, shards(): pl.pallas_call(kernel, out_shape=(jax.ShapeDtypeStruct((128, 1792), BF16)...  134 us
    pallas_call x1, Pallas kernels, shards(): pl.pallas_call(copy_kernel, out_shape=(jax.ShapeDtypeStruct((128, 1792),...  4.13 us

profile of v7, /device:TPU:32, one launch (start us, length us, event | category | flops | bytes accessed | tf_op | source)
XLA Modules:
  0.0 139.1 jit_solution(13717358116166820102)
XLA Ops:
  0.6 134.3 %shard_map.93 = (bf16[128,1792]{1,0:T(8,128)(2,1)}, bf16[128,1792]{1,0:T(8,128)(2,1)}, f32[1792,512]{1,0:T(8,128)}, f32[7,512]{1,0:T(8,128)}) custom-call(bf16[128,8192]{1,0:T(8,128)(2,1)} %dy_ref.1, bf16[128,1792]{1,0:T(8,128)(2,1)} %gate_in.1, bf16[128,1792]{1,0:T(8,128)(2,1)} %up_in.1, bf16[1792,512]{1,0:T(8,128)(2,1)} %dw_in.1, f32[7,512]{1,0:T(8,128)} %step_in.1, ...), custom_call_target="tpu_custom_call" | custom-call | flops 8000000000 | bytes 12000000 | tf_op jit(solution)/shard_map/pallas_call | solution.py:505
  135.0 4.1 %shard_map.94 = (bf16[128,1792]{1,0:T(8,128)(2,1)}, bf16[128,1792]{1,0:T(8,128)(2,1)}, f32[1792,512]{1,0:T(8,128)}, f32[7,512]{1,0:T(8,128)}) custom-call(bf16[128,1792]{1,0:T(8,128)(2,1)} %get-tuple-element.8.dgate_in, bf16[128,1792]{1,0:T(8,128)(2,1)} %get-tuple-element.9.dup_in, f32[1792,512]{1,0:T(8,128)} %get-tuple-element.10.wg_in, ...), custom_call_target="tpu_custom_call" | custom-call | bytes 10000000 | tf_op jit(solution)/shard_map/pallas_call | solution.py:564
